TPU v7x, 32 devices: a whole 2x2x4 slice. The times are simulated.
32 devices in a mesh: group: 8 (over z, core), sub: 4 (over y, x).
Axes of the slice: x: 2, y: 2, z: 4, core: 2. Of those that a mesh axis runs over, the one named last changes fastest.
Arguments:
- points: bfloat16 [32768, 768], P(('group', 'sub')), may hold values from -6 to 6
- anchors: bfloat16 [256, 768], replicated, may hold values from -6 to 6
- neighbours: int32 [64, 4], P(('group', 'sub')), may hold values from 0 to 63, as said below
Outputs:
- near_blocks: float32 [32768, 4, 512], P(('group', 'sub'))
- leaf_basis: bfloat16 [32768, 256], P(('group', 'sub'))
- transfer: float32 [32, 2, 256, 256], P(('group', 'sub'))
- coupling: float32 [32, 2, 256, 256], P(('group', 'sub'))
Inputs may be any that keep to these rules, and one draw needn't show every extreme that they name: Each leaf's 4 neighbours are different leaves at cyclic distance 1, 2 or 3 from it in the order of leaf numbers modulo 64.
All inputs are finite; a program needn't handle non-finite values.
Results may differ from a plain program's by a relative error of at most 0.0077.
Values may be sent and summed in bfloat16 or wider, within the bound.
A program may use at most 128 MiB of HBM per device.

v0:
```python
import math

import jax
import jax.numpy as jnp
from jax import lax
from jax.sharding import PartitionSpec as P

LEAF = 512


def from_behind(value, axis, steps):
    count = lax.axis_size(axis)
    pairs = [(source, (source + steps) % count) for source in range(count)]
    return lax.ppermute(value, axis, pairs)


def from_partner(block, axis, stride):
    count = lax.axis_size(axis)
    route = []
    for low in range(count):
        high = low | 1 << stride
        if high != low and high < count:
            route += [(low, high), (high, low)]
    return lax.ppermute(block, axis, route)


def unit_rows(values):
    wide = values.astype(jnp.float32)
    scale = lax.rsqrt(jnp.sum(wide * wide, axis=-1, keepdims=True) + 1e-06)
    return (wide * scale).astype(jnp.bfloat16)


def lower_solve(factor, right):
    return lax.linalg.triangular_solve(factor, right, left_side=True, lower=True)


def swap_last(matrix):
    return jnp.swapaxes(matrix, -1, -2)


def shards(points, anchors, neighbours):
    leaves_dev = neighbours.shape[0]
    width = points.shape[1]
    rank = anchors.shape[0]
    beta = 0.5 * math.sqrt(width)
    unit = unit_rows(points)
    anchor_unit = unit_rows(anchors)
    leaves = unit.reshape(leaves_dev, LEAF, width)
    reach = 3
    lower_parts = []
    upper_parts = []
    plan = []
    for step in range(1, (reach + leaves_dev - 1) // leaves_dev + 1):
        count = min(leaves_dev, reach - (step - 1) * leaves_dev)
        plan.append((leaves[leaves_dev - count :], step))
        plan.append((leaves[:count], -step))
    for piece, step in plan:
        got = from_behind(piece, ("group", "sub"), step)
        if step > 0:
            lower_parts.insert(0, got)
        else:
            upper_parts.append(got)
    window = jnp.concatenate(lower_parts + [leaves] + upper_parts, axis=0)
    total_leaves = leaves_dev * lax.axis_size(("group", "sub"))
    first_leaf = lax.axis_index(("group", "sub")) * leaves_dev
    local = jnp.arange(leaves_dev, dtype=jnp.int32)[:, None]
    offsets = jnp.remainder(neighbours - first_leaf - local + reach, total_leaves) - reach
    picks = reach + local + offsets
    cols = jnp.take(window, picks, axis=0)
    scores = jnp.einsum("apd,akqd->apkq", leaves, cols, preferred_element_type=jnp.float32)
    near_blocks = jnp.exp(beta * scores).reshape(leaves_dev * LEAF, neighbours.shape[1], LEAF)
    sketch = jnp.exp(beta * jnp.dot(unit, anchor_unit.T, preferred_element_type=jnp.float32))
    sketch = sketch.reshape(leaves_dev, LEAF, rank)
    grams = jnp.einsum("lpr,lps->lrs", sketch, sketch, precision=lax.Precision.HIGHEST) / LEAF
    factors = jnp.linalg.cholesky(grams)
    basis = swap_last(lower_solve(factors, swap_last(sketch)))
    leaf_basis = basis.reshape(leaves_dev * LEAF, rank).astype(jnp.bfloat16)
    node = jnp.sum(grams, axis=0) / leaves_dev
    node_factor = jnp.linalg.cholesky(node)
    levels = lax.axis_size("sub").bit_length() - 1
    transfers = []
    couplings = []
    for level in range(levels):
        partner = from_partner(node, "sub", level)
        parent = (node + partner) * 0.5
        partner_factor = jnp.linalg.cholesky(partner)
        parent_factor = jnp.linalg.cholesky(parent)
        transfers.append(swap_last(lower_solve(parent_factor, node_factor)))
        couplings.append(lower_solve(node_factor, partner_factor))
        node = parent
        node_factor = parent_factor
    transfer = jnp.stack(transfers, axis=0)[None]
    coupling = jnp.stack(couplings, axis=0)[None]
    return (near_blocks, leaf_basis, transfer, coupling)


def solution(mesh):
    return jax.shard_map(
        shards,
        mesh=mesh,
        in_specs=(P(("group", "sub"), None), P(), P(("group", "sub"), None)),
        out_specs=(
            P(("group", "sub"), None, None),
            P(("group", "sub"), None),
            P(("group", "sub"), None, None, None),
            P(("group", "sub"), None, None, None),
        ),
        check_vma=False,
    )
```

profile of v0, /device:TPU:0, one launch (start us, length us, event | category | flops | bytes accessed | tf_op | source)
XLA Modules:
  0.0 480.9 jit_solution(2950889262544348513)
XLA Ops:
  7.2 3.5 collective-permute-start.2
  17.5 4.6 collective-permute-start.3
  29.2 11.7 %cholesky.412 = f32[128,128]{1,0:T(8,128)S(1)} custom-call(f32[128,128]{1,0:T(8,128)S(1)} %cholesky.550), custom_call_target="Cholesky" | custom-call | tf_op jit(solution)/shard_map/jit(cholesky)/cholesky | solution.py:79
  41.5 10.4 %custom-call.39 = f32[1,128,128]{1,2,0:T(8,128)} custom-call(f32[1,128,128]{2,1,0:T(8,128)S(1)} %get-tuple-element.118), custom_call_target="InvertDiagBlocksLowerTriangular" | custom-call | tf_op jit(solution)/shard_map/jit(cholesky)/cholesky | solution.py:79
  55.5 11.7 %cholesky.429 = f32[128,128]{1,0:T(8,128)S(1)} custom-call(f32[128,128]{1,0:T(8,128)S(1)} %convolution_subtract_fusion.7), custom_call_target="Cholesky" | custom-call | tf_op jit(solution)/shard_map/jit(cholesky)/cholesky | solution.py:79
  73.5 7.5 %while.12 = (s32[]{:T(128)}, f32[256,256]{1,0:T(8,128)}, s32[2,2]{1,0:T(2,128)}, f32[2,128,128]{2,1,0:T(8,128)S(1)}, s32[]{:T(128)}) while((s32[]{:T(128)}, f32[256,256]{1,0:T(8,128)}, s32[2,2]{1,0:T(2,128)}, f32[2,128,128]{2,1,0:T(8,128)S(1)}, s32[]{:T(128)}) %tuple.113), condition=%wide.while_cond.clone.1, body=%wide.while_body.clone.1.sunk | while | flops 2 | bytes 131181 | solution.py:34
  81.1 20.3 %custom-call.44 = f32[2,128,128]{1,2,0:T(8,128)} custom-call(f32[2,128,128]{2,1,0:T(8,128)S(1)} %get-tuple-element.42), custom_call_target="InvertDiagBlocksLowerTriangular" | custom-call | tf_op jit(solution)/shard_map/triangular_solve/custom-call.7 | solution.py:34
  104.3 23.5 %custom-call.27 = f32[2,128,128]{2,1,0:T(8,128)S(1)} custom-call(f32[2,128,128]{2,1,0:T(8,128)S(1)} %cholesky.544), custom_call_target="Cholesky" | custom-call | tf_op jit(solution)/shard_map/jit(cholesky)/cholesky | solution.py:75
  129.1 21.1 %custom-call.28 = f32[2,1,128,128]{2,3,1,0:T(8,128)} custom-call(f32[2,1,128,128]{3,2,1,0:T(8,128)} %select_bitcast_fusion), custom_call_target="InvertDiagBlocksLowerTriangular" | custom-call | tf_op jit(solution)/shard_map/jit(cholesky)/cholesky | solution.py:75
  153.4 24.9 %custom-call.29 = f32[2,128,128]{2,1,0:T(8,128)} custom-call(f32[2,128,128]{2,1,0:T(8,128)} %convolution_subtract_fusion.5), custom_call_target="Cholesky" | custom-call | tf_op jit(solution)/shard_map/jit(cholesky)/cholesky | solution.py:75
  181.3 6.6 %while.9 = (s32[]{:T(128)}, f32[2,256,256]{2,1,0:T(8,128)S(1)}, s32[2,2]{1,0:T(2,128)}, f32[2,2,128,128]{3,2,0,1:T(8,128)}, s32[]{:T(128)}) while((s32[]{:T(128)}, f32[2,256,256]{2,1,0:T(8,128)S(1)}, s32[2,2]{1,0:T(2,128)}, f32[2,2,128,128]{3,2,0,1:T(8,128)}, s32[]{:T(128)}) %tuple.116), condition=%wide.while_cond.1, body=%wide.while_body.1.sunk | while | flops 2 | bytes 263777 | solution.py:34
  187.9 40.9 %custom-call.30 = f32[2,2,128,128]{2,3,1,0:T(8,128)} custom-call(f32[2,2,128,128]{3,2,1,0:T(8,128)} %bitcast.213), custom_call_target="InvertDiagBlocksLowerTriangular" | custom-call | tf_op jit(solution)/shard_map/triangular_solve | solution.py:34
  237.1 11.7 %cholesky.480 = f32[128,128]{1,0:T(8,128)S(1)} custom-call(f32[128,128]{1,0:T(8,128)S(1)} %cholesky.556), custom_call_target="Cholesky" | custom-call | tf_op jit(solution)/shard_map/jit(cholesky)/cholesky | solution.py:86
  248.8 9.8 %custom-call.43 = f32[1,128,128]{1,2,0:T(8,128)S(1)} custom-call(f32[1,128,128]{2,1,0:T(8,128)S(1)} %get-tuple-element.110), custom_call_target="InvertDiagBlocksLowerTriangular" | custom-call | tf_op jit(solution)/shard_map/jit(cholesky)/cholesky | solution.py:86
  259.2 12.1 %cholesky.497 = f32[128,128]{1,0:T(8,128)S(1)} custom-call(f32[128,128]{1,0:T(8,128)S(1)} %slice_subtract_fusion.1), custom_call_target="Cholesky" | custom-call | tf_op jit(solution)/shard_map/jit(cholesky)/cholesky | solution.py:86
  275.1 11.7 %cholesky.378 = f32[128,128]{1,0:T(8,128)S(1)} custom-call(f32[128,128]{1,0:T(8,128)S(1)} %cholesky.547), custom_call_target="Cholesky" | custom-call | tf_op jit(solution)/shard_map/jit(cholesky)/cholesky | solution.py:87
  286.8 9.8 %custom-call.38 = f32[1,128,128]{1,2,0:T(8,128)S(1)} custom-call(f32[1,128,128]{2,1,0:T(8,128)S(1)} %get-tuple-element.126), custom_call_target="InvertDiagBlocksLowerTriangular" | custom-call | tf_op jit(solution)/shard_map/jit(cholesky)/cholesky | solution.py:87
  297.2 11.7 %cholesky.395 = f32[128,128]{1,0:T(8,128)S(1)} custom-call(f32[128,128]{1,0:T(8,128)S(1)} %convolution_subtract_fusion.8), custom_call_target="Cholesky" | custom-call | tf_op jit(solution)/shard_map/jit(cholesky)/cholesky | solution.py:87
  311.9 4.0 while.10
  315.9 19.8 %custom-call.40 = f32[2,128,128]{1,2,0:T(8,128)S(1)} custom-call(f32[2,128,128]{2,1,0:T(8,128)S(1)} %get-tuple-element.40), custom_call_target="InvertDiagBlocksLowerTriangular" | custom-call | tf_op jit(solution)/shard_map/triangular_solve/custom-call.7 | solution.py:34
  338.3 11.7 %cholesky.514 = f32[128,128]{1,0:T(8,128)S(1)} custom-call(f32[128,128]{1,0:T(8,128)S(1)} %cholesky.559), custom_call_target="Cholesky" | custom-call | tf_op jit(solution)/shard_map/jit(cholesky)/cholesky | solution.py:86
  350.0 9.8 %custom-call.45 = f32[1,128,128]{1,2,0:T(8,128)S(1)} custom-call(f32[1,128,128]{2,1,0:T(8,128)S(1)} %get-tuple-element.114), custom_call_target="InvertDiagBlocksLowerTriangular" | custom-call | tf_op jit(solution)/shard_map/jit(cholesky)/cholesky | solution.py:86
  360.4 12.3 %cholesky.531 = f32[128,128]{1,0:T(8,128)} custom-call(f32[128,128]{1,0:T(8,128)S(1)} %slice_subtract_fusion), custom_call_target="Cholesky" | custom-call | tf_op jit(solution)/shard_map/jit(cholesky)/cholesky | solution.py:86
  373.0 11.9 %cholesky.446 = f32[128,128]{1,0:T(8,128)S(1)} custom-call(f32[128,128]{1,0:T(8,128)S(1)} %cholesky.553), custom_call_target="Cholesky" | custom-call | tf_op jit(solution)/shard_map/jit(cholesky)/cholesky | solution.py:87
  384.9 9.8 %custom-call.41 = f32[1,128,128]{1,2,0:T(8,128)S(1)} custom-call(f32[1,128,128]{2,1,0:T(8,128)S(1)} %get-tuple-element.122), custom_call_target="InvertDiagBlocksLowerTriangular" | custom-call | tf_op jit(solution)/shard_map/jit(cholesky)/cholesky | solution.py:87
  395.2 11.7 %cholesky.463 = f32[128,128]{1,0:T(8,128)S(1)} custom-call(f32[128,128]{1,0:T(8,128)S(1)} %convolution_subtract_fusion.6), custom_call_target="Cholesky" | custom-call | tf_op jit(solution)/shard_map/jit(cholesky)/cholesky | solution.py:87
  408.9 3.8 while.11
  412.8 19.9 %custom-call.42 = f32[2,128,128]{1,2,0:T(8,128)S(1)} custom-call(f32[2,128,128]{2,1,0:T(8,128)S(1)} %get-tuple-element.41), custom_call_target="InvertDiagBlocksLowerTriangular" | custom-call | tf_op jit(solution)/shard_map/triangular_solve/custom-call.7 | solution.py:34
  451.8 6.4 %gather_fusion = bf16[8,512,768]{2,1,0:T(8,128)(2,1)} fusion(bf16[8,512,768]{2,1,0:T(8,128)(2,1)} %constant_dynamic-update-slice_fusion, s32[1024]{0:T(1024)S(1)} %pad_clamp_fusion), kind=kCustom, calls=%fused_computation | custom fusion | bytes 12582944 | tf_op jit(solution)/shard_map/jit(_take)/gather | solution.py:69
  458.2 5.9 %multiply_exponential_fusion = f32[2,512,4,512]{3,1,2,0:T(8,128)S(1)} fusion(bf16[2,512,768,1]{2,1,3,0:T(8,128)(2,1)S(1)} %bitcast.206, bf16[2,4,512,768]{3,2,1,0:T(8,128)(2,1)} %bitcast.209, pred[2,4]{1,0:T(4,128)(4,1)S(1)} %get-tuple-element.94), kind=kOutput, calls=%fused_computation.9 | convolution fusion | flops 3226468352 | bytes 16252936 | tf_op jit(solution)/shard_map/apd,akqd->apkq/dot_general | solution.py:70
  464.1 4.3 copy.40
  468.3 12.2 %copy.56 = f32[1024,4,512]{2,1,0:T(4,128)} copy(f32[1024,4,512]{2,0,1:T(8,128)} %bitcast.202) | data formatting | bytes 16777216
  (169 shorter events, 97.0 us)
Async XLA Ops:
  4.2 439.0 %collective-permute-start.1 = (bf16[2,512,768]{2,1,0:T(8,128)(2,1)S(1)}, bf16[2,512,768]{2,1,0:T(8,128)(2,1)}, u32[]{:S(2)}, u32[]{:S(2)}) collective-permute-start(bf16[2,512,768]{2,1,0:T(8,128)(2,1)S(1)} %bitcast.203), channel_id=1, source_target_pairs={{0,1},{1,2},{2,3},{3,4},{4,5},{5,6},{6,7},{7,8},{8,9},{9,10},{10,1... | collective-permute-start | bytes 4718600 | tf_op jit(solution)/shard_map/ppermute | solution.py:14
  7.2 439.9 %collective-permute-start.2 = (bf16[2,512,768]{2,1,0:T(8,128)(2,1)S(1)}, bf16[2,512,768]{2,1,0:T(8,128)(2,1)}, u32[]{:S(2)}, u32[]{:S(2)}) collective-permute-start(bf16[2,512,768]{2,1,0:T(8,128)(2,1)S(1)} %bitcast.204), channel_id=1, source_target_pairs={{0,31},{1,0},{2,1},{3,2},{4,3},{5,4},{6,5},{7,6},{8,7},{9,8},{10,9... | collective-permute-start | bytes 4718600 | tf_op jit(solution)/shard_map/ppermute | solution.py:14
  16.1 217.7 %collective-permute-start.4 = (f32[256,256]{0,1:T(8,128)}, f32[256,256]{0,1:T(8,128)}, u32[]{:S(2)}, u32[]{:S(2)}) collective-permute-start(f32[256,256]{0,1:T(8,128)} %broadcast_multiply_fusion), channel_id=1, source_target_pairs={{0,1},{1,0},{2,3},{3,2},{4,5},{5,4},{6,7},{7,6},{8,9},{9,8},{10,11... | collective-permute-start | bytes 786440 | tf_op jit(solution)/shard_map/ppermute | solution.py:24
  17.4 423.7 %collective-permute-start = (bf16[1,512,768]{2,1,0:T(8,128)(2,1)}, bf16[1,512,768]{2,1,0:T(8,128)(2,1)}, u32[]{:S(2)}, u32[]{:S(2)}) collective-permute-start(bf16[1,512,768]{2,1,0:T(8,128)(2,1)} %get-tuple-element.105), channel_id=1, source_target_pairs={{0,2},{1,3},{2,4},{3,5},{4,6},{5,7},{6,8},{7,9},{8,10},{9,11},{10,... | collective-permute-start | bytes 2359304 | tf_op jit(solution)/shard_map/ppermute | solution.py:14
  17.5 432.3 %collective-permute-start.3 = (bf16[1,512,768]{2,1,0:T(8,128)(2,1)}, bf16[1,512,768]{2,1,0:T(8,128)(2,1)}, u32[]{:S(2)}, u32[]{:S(2)}) collective-permute-start(bf16[1,512,768]{2,1,0:T(8,128)(2,1)} %get-tuple-element.104), channel_id=1, source_target_pairs={{0,30},{1,31},{2,0},{3,1},{4,2},{5,3},{6,4},{7,5},{8,6},{9,7},{10,... | collective-permute-start | bytes 2359304 | tf_op jit(solution)/shard_map/ppermute | solution.py:14
  26.9 201.9 %copy-start = (f32[2,512,256]{1,2,0:T(8,128)S(1)}, f32[2,512,256]{1,2,0:T(8,128)}, u32[]{:S(2)}) copy-start(f32[2,512,256]{1,2,0:T(8,128)} %copy.47) | copy-start | bytes 3145732
  28.5 0.7 copy-start.5
  103.4 0.8 copy-start.2
  179.3 0.8 copy-start.1
  179.3 54.3 %copy-start.7 = (s32[2,4]{1,0:T(2,128)S(1)}, s32[2,4]{1,0:T(2,128)}, u32[]{:S(2)}) copy-start(s32[2,4]{1,0:T(2,128)} %param.8) | copy-start | bytes 100
  179.3 54.3 %copy-start.8 = (s32[2]{0:T(128)S(1)}, s32[2]{0:T(128)}, u32[]{:S(2)}) copy-start(s32[2]{0:T(128)} %iota_add_fusion) | copy-start | bytes 28
  181.3 92.0 %copy-start.6 = (f32[2,128,128]{1,2,0:T(8,128)S(1)}, f32[2,128,128]{1,2,0:T(8,128)}, u32[]{:S(2)}) copy-start(f32[2,128,128]{1,2,0:T(8,128)} %custom-call.44) | copy-start | bytes 393220
  230.4 81.5 %copy-start.9 = (s32[2,2]{1,0:T(2,128)S(1)}, s32[2,2]{1,0:T(2,128)}, u32[]{:S(2)}) copy-start(s32[2,2]{1,0:T(2,128)} %get-tuple-element.340) | copy-start | bytes 52
  231.0 104.8 %copy-start.3 = (f32[256,256]{1,0:T(8,128)S(1)}, f32[256,256]{1,0:T(8,128)}, u32[]{:S(2)}) copy-start(f32[256,256]{1,0:T(8,128)} %get-tuple-element.91) | copy-start | bytes 786436
  234.8 103.3 %collective-permute-start.5 = (f32[256,256]{0,1:T(8,128)S(1)}, f32[256,256]{0,1:T(8,128)S(1)}, u32[]{:S(2)}, u32[]{:S(2)}) collective-permute-start(f32[256,256]{0,1:T(8,128)S(1)} %add_multiply_fusion.1), channel_id=1, source_target_pairs={{0,2},{2,0},{1,3},{3,1},{4,6},{6,4},{5,7},{7,5},{8,10},{10,8},{9,1... | collective-permute-start | bytes 786440 | tf_op jit(solution)/shard_map/ppermute | solution.py:24
  308.9 1.9 copy-start.4
where the time goes:
time: 486 us; the launch traced here: 481 us
  other arithmetic  368 us (76%)
  local copies, waits for them, and re-layouts  68.1 us (14%)
  matrix products  25.3 us (5%)
  starting transfers between devices  11.2 us (2%)
  between operations  8.05 us (2%)
    another operation x10, other arithmetic, lower_solve(): lax.linalg.triangular_solve(factor, right, left_side=True, lower=True)  106 us
    another operation x9, other arithmetic, shards(): factors = jnp.linalg.cholesky(grams)  72.6 us
    another operation x12, other arithmetic, shards(): partner_factor = jnp.linalg.cholesky(partner)  69.7 us
    another operation x12, other arithmetic, shards(): parent_factor = jnp.linalg.cholesky(parent)  68.1 us
    another operation x6, other arithmetic, shards(): node_factor = jnp.linalg.cholesky(node)  36.4 us
    unnamed x26, local copies, waits for them, and re-layouts  23.9 us
    another operation x19, local copies, waits for them, and re-layouts, lower_solve(): lax.linalg.triangular_solve(factor, right, left_side=True, lower=True)  16 us
    ppermute x4, starting transfers between devices, from_behind(): return lax.ppermute(value, axis, pairs)  11.1 us
  transfers between devices with their start and end apart: 6, of which 0 were waited for; matrix products, arithmetic and copies ran while one was open for 88% of the time, Pallas kernels for 0%

commit v1 on v0

v1 whole, which is shorter than its diff:
```python
import functools
import math

import jax
import jax.numpy as jnp
from jax import lax
from jax.experimental import pallas as pl
from jax.experimental.pallas import tpu as pltpu
from jax.sharding import PartitionSpec as P

LEAF = 512
PANEL = 32
HIGHEST = lax.Precision.HIGHEST


def from_behind(value, axis, steps):
    count = lax.axis_size(axis)
    pairs = [(source, (source + steps) % count) for source in range(count)]
    return lax.ppermute(value, axis, pairs)


def from_partner(block, axis, stride):
    count = lax.axis_size(axis)
    route = []
    for low in range(count):
        high = low | 1 << stride
        if high != low and high < count:
            route += [(low, high), (high, low)]
    return lax.ppermute(block, axis, route)


def unit_rows(values):
    wide = values.astype(jnp.float32)
    scale = lax.rsqrt(jnp.sum(wide * wide, axis=-1, keepdims=True) + 1e-06)
    return (wide * scale).astype(jnp.bfloat16)


def split3(x):
    a = x.astype(jnp.bfloat16)
    rest = x - a.astype(jnp.float32)
    b = rest.astype(jnp.bfloat16)
    c = (rest - b.astype(jnp.float32)).astype(jnp.bfloat16)
    return a, b, c


def factor_kernel(count, rank, grams_ref, upper_ref, inverse_ref, work, *blocks):
    b = PANEL
    eye_row = lax.broadcasted_iota(jnp.int32, (rank, rank), 0)
    eye_col = lax.broadcasted_iota(jnp.int32, (rank, rank), 1)
    eye = jnp.where(eye_row == eye_col, 1.0, 0.0).astype(jnp.float32)
    for m in range(count):
        work[m, :, :rank] = grams_ref[m]
        work[m, :, rank:] = eye
    for block in blocks:
        block[...] = jnp.ones_like(block)
    lane = lax.broadcasted_iota(jnp.int32, (b, 128), 1)
    row = lax.broadcasted_iota(jnp.int32, (b, 128), 0)
    unit_part = jnp.where(lane == row + b, 1.0, 0.0).astype(jnp.float32)
    panel_row = lax.broadcasted_iota(jnp.int32, (b, rank), 0)
    panel_col = lax.broadcasted_iota(jnp.int32, (b, rank), 1)

    def panel(step, carry):
        start = pl.multiple_of(step * b, b)
        for m in range(count):
            rows = work[m, pl.ds(start, b), :rank]
            rolled = pltpu.roll(rows, rank - start, 1)[:, :128]
            blocks[m // 8][pl.ds(m % 8, b, stride=8), :] = jnp.where(lane < b, rolled, unit_part)
        for block in blocks:
            v = [block[r * 8:(r + 1) * 8, :] for r in range(b)]
            for k in range(b):
                pivot = jnp.broadcast_to(v[k][:, k:k + 1], (8, 128))
                scaled = v[k] * (1.0 / pivot)
                for i in range(k + 1, b):
                    v[i] = v[i] - jnp.broadcast_to(v[k][:, i:i + 1], (8, 128)) * scaled
                block[k * 8:(k + 1) * 8, :] = v[k] * lax.rsqrt(pivot)
        for m in range(count):
            small = blocks[m // 8][pl.ds(m % 8, b, stride=8), :][:, b:2 * b]
            reduced = jnp.dot(small, work[m, pl.ds(start, b), :], precision=HIGHEST, preferred_element_type=jnp.float32)
            left = jnp.where(panel_col >= start + panel_row, reduced[:, :rank], 0.0)
            work[m, pl.ds(start, b), :rank] = left
            work[m, pl.ds(start, b), rank:] = reduced[:, rank:]
            full = jnp.concatenate([left, reduced[:, rank:]], axis=1)
            y1, y2, y3 = split3(full)
            x1, x2, x3 = split3(jnp.where(panel_col >= start + b, left, 0.0))
            lhs = jnp.concatenate([x1, x1, x2, x2, x1, x3], axis=0)
            rhs = jnp.concatenate([y1, y2, y1, y2, y3, y1], axis=0)
            work[m] = work[m] - lax.dot_general(lhs, rhs, (((0,), (0,)), ((), ())), preferred_element_type=jnp.float32)
        return carry

    lax.fori_loop(0, rank // b, panel, 0)
    for m in range(count):
        upper_ref[m] = work[m, :, :rank]
        inverse_ref[m] = work[m, :, rank:]


def factors_of(grams):
    count, rank, _ = grams.shape
    shape = jax.ShapeDtypeStruct((count, rank, rank), jnp.float32)
    vmem = pl.BlockSpec(memory_space=pltpu.VMEM)
    return pl.pallas_call(
        functools.partial(factor_kernel, count, rank),
        out_shape=(shape, shape),
        in_specs=[vmem],
        out_specs=(vmem, vmem),
        scratch_shapes=[pltpu.VMEM((count, rank, 2 * rank), jnp.float32)]
        + [pltpu.VMEM((8 * PANEL, 128), jnp.float32)] * ((count + 7) // 8),
        compiler_params=pltpu.CompilerParams(vmem_limit_bytes=40 << 20),
        cost_estimate=pl.CostEstimate(flops=40_000_000_000, bytes_accessed=8_000_000, transcendentals=0),
        name="factor",
    )(grams)


def near_kernel(beta, picks_ref, *refs):
    *parts, rows_ref, out_ref, window, sems = refs
    leaf = pl.program_id(0)

    @pl.when((leaf == 0) & (pl.program_id(1) == 0))
    def _():
        at = 0
        copies = []
        for n, part in enumerate(parts):
            size = part.shape[0]
            copies.append(pltpu.make_async_copy(part, window.at[pl.ds(at, size)], sems.at[n]))
            at += size
        for copy in copies:
            copy.start()
        for copy in copies:
            copy.wait()

    rows = rows_ref[0]
    for j in range(out_ref.shape[1]):
        cols = window[picks_ref[leaf, j]]
        scores = lax.dot_general(rows, cols, (((1,), (1,)), ((), ())), preferred_element_type=jnp.float32)
        out_ref[:, j, :] = jnp.exp(beta * scores)


def near_field(parts, leaves, picks, beta):
    leaves_dev, leaf, width = leaves.shape
    nbr = picks.shape[1]
    chunk = 256
    steps = leaf // chunk
    total = sum(part.shape[0] for part in parts)
    return pl.pallas_call(
        functools.partial(near_kernel, beta),
        out_shape=jax.ShapeDtypeStruct((leaves_dev * leaf, nbr, leaf), jnp.float32),
        grid_spec=pltpu.PrefetchScalarGridSpec(
            num_scalar_prefetch=1,
            grid=(leaves_dev, steps),
            in_specs=[pl.BlockSpec(memory_space=pl.ANY)] * len(parts)
            + [pl.BlockSpec((1, chunk, width), lambda a, c, p: (a, c, 0))],
            out_specs=pl.BlockSpec((chunk, nbr, leaf), lambda a, c, p: (a * steps + c, 0, 0)),
            scratch_shapes=[
                pltpu.VMEM((total, leaf, width), jnp.bfloat16),
                pltpu.SemaphoreType.DMA((len(parts),)),
            ],
        ),
        compiler_params=pltpu.CompilerParams(vmem_limit_bytes=40 << 20),
        cost_estimate=pl.CostEstimate(flops=4_000_000_000, bytes_accessed=16_000_000, transcendentals=2_000_000),
        name="near",
    )(picks, *parts, leaves)


def shards(points, anchors, neighbours):
    leaves_dev = neighbours.shape[0]
    width = points.shape[1]
    rank = anchors.shape[0]
    beta = 0.5 * math.sqrt(width)
    unit = unit_rows(points)
    anchor_unit = unit_rows(anchors)
    leaves = unit.reshape(leaves_dev, LEAF, width)
    reach = 3
    lower_parts = []
    upper_parts = []
    plan = []
    for step in range(1, (reach + leaves_dev - 1) // leaves_dev + 1):
        count = min(leaves_dev, reach - (step - 1) * leaves_dev)
        plan.append((leaves[leaves_dev - count :], step))
        plan.append((leaves[:count], -step))
    for piece, step in plan:
        got = from_behind(piece, ("group", "sub"), step)
        if step > 0:
            lower_parts.insert(0, got)
        else:
            upper_parts.append(got)

    sketch = jnp.exp(beta * jnp.dot(unit, anchor_unit.T, preferred_element_type=jnp.float32))
    sketch = sketch.reshape(leaves_dev, LEAF, rank)
    grams = jnp.einsum("lpr,lps->lrs", sketch, sketch, precision=HIGHEST) / LEAF
    node = jnp.sum(grams, axis=0) / leaves_dev
    levels = lax.axis_size("sub").bit_length() - 1
    stack = [grams[leaf] for leaf in range(leaves_dev)] + [node]
    for level in range(levels):
        partner = from_partner(node, "sub", level)
        node = (node + partner) * 0.5
        stack += [partner, node]
    upper, inverse = factors_of(jnp.stack(stack, axis=0))
    basis = jnp.einsum("lpr,lsr->lps", sketch, inverse[:leaves_dev], precision=HIGHEST)
    leaf_basis = basis.reshape(leaves_dev * LEAF, rank).astype(jnp.bfloat16)
    own = slice(leaves_dev, leaves_dev + 2 * levels, 2)
    sibling = slice(leaves_dev + 1, leaves_dev + 1 + 2 * levels, 2)
    parent = slice(leaves_dev + 2, leaves_dev + 2 + 2 * levels, 2)
    transfer = jnp.einsum("tij,tkj->tik", upper[own], inverse[parent], precision=HIGHEST)[None]
    coupling = jnp.einsum("tij,tkj->tik", inverse[own], upper[sibling], precision=HIGHEST)[None]

    total_leaves = leaves_dev * lax.axis_size(("group", "sub"))
    first_leaf = lax.axis_index(("group", "sub")) * leaves_dev
    local = jnp.arange(leaves_dev, dtype=jnp.int32)[:, None]
    offsets = jnp.remainder(neighbours - first_leaf - local + reach, total_leaves) - reach
    picks = reach + local + offsets
    near_blocks = near_field(lower_parts + [leaves] + upper_parts, leaves, picks, beta)
    return (near_blocks, leaf_basis, transfer, coupling)


def solution(mesh):
    return jax.shard_map(
        shards,
        mesh=mesh,
        in_specs=(P(("group", "sub"), None), P(), P(("group", "sub"), None)),
        out_specs=(
            P(("group", "sub"), None, None),
            P(("group", "sub"), None),
            P(("group", "sub"), None, None, None),
            P(("group", "sub"), None, None, None),
        ),
        check_vma=False,
    )
```

time: 486 us -> 161 us (0.33)
  other arithmetic: 368 us -> 5.72 us
  waiting for transfers between devices: 0.02 us -> 74 us
  local copies, waits for them, and re-layouts: 68.1 us -> 3.71 us
  Pallas kernels: 0 us -> 56.7 us
  matrix products: 25.3 us -> 8.19 us
  between operations: 8.05 us -> 0.74 us
    another operation x53 -> x1, other arithmetic: 354 us -> 1.69 us  [shards(): upper, inverse = factors_of(jnp.stack(stack, axis=0))]
    ppermute x2, waiting for transfers between devices: 0.01 us -> 74 us  [from_partner(): return lax.ppermute(block, axis, route)]
    pallas_call x0 -> x2, Pallas kernels: none -> 56.7 us  [the longest x1 47.8 us: factors_of(): pl.pallas_call(functools.partial(factor_kernel, count, rank), out_shape=(...]
    another operation x40 -> x0, local copies, waits for them, and re-layouts: 23.6 us -> none  [the longest x19 16 us: lower_solve(): lax.linalg.triangular_solve(factor, right, left_side=True, lower=True)]
    unnamed x26 -> x12, local copies, waits for them, and re-layouts: 23.9 us -> 2.43 us
    another operation x27 -> x0, matrix products: 15.9 us -> none  [the longest x15 8.04 us: lower_solve(): lax.linalg.triangular_solve(factor, right, left_side=True, lower=True)]
    gather x1 -> x0, local copies, waits for them, and re-layouts: 6.39 us -> none  [shards(): cols = jnp.take(window, picks, axis=0)]
  transfers between devices with their start and end apart: 6 -> 6, of which waited for: 0 -> 2; matrix products, arithmetic and copies ran while one was open for 88% -> 9% of each run, Pallas kernels for 0% -> 30%
where the time goes in v1:
time: 161 us; the launch traced here: 160 us
  waiting for transfers between devices  74 us (46%)
  Pallas kernels  56.7 us (35%)
  starting transfers between devices  11.4 us (7%)
  matrix products  8.19 us (5%)
  other arithmetic  5.72 us (4%)
  local copies, waits for them, and re-layouts  3.71 us (2%)
    ppermute x2, waiting for transfers between devices, from_partner(): return lax.ppermute(block, axis, route)  74 us
    pallas_call x1, Pallas kernels, factors_of(): pl.pallas_call(functools.partial(factor_kernel, count, rank), out_shape=(...  47.8 us
    ppermute x4, starting transfers between devices, from_behind(): return lax.ppermute(value, axis, pairs)  10.9 us
    pallas_call x1, Pallas kernels, near_field(): pl.pallas_call(functools.partial(near_kernel, beta), out_shape=jax.ShapeD...  8.85 us
  transfers between devices with their start and end apart: 6, of which 2 were waited for; matrix products, arithmetic and copies ran while one was open for 9% of the time, Pallas kernels for 30%

profile of v1, /device:TPU:0, one launch (start us, length us, event | category | flops | bytes accessed | tf_op | source)
XLA Modules:
  0.0 160.4 jit_solution(12890271651668281715)
XLA Ops:
  0.6 1.9 %fusion = f32[1024]{0:T(1024)S(1)} fusion(bf16[1024,768]{1,0:T(8,128)(2,1)} %param.3), kind=kLoop, calls=%fused_computation.2 | loop fusion | flops 2358272 | bytes 1576960 | tf_op jit(solution)/shard_map/reduce_sum | solution.py:34
  2.5 0.0 copy-start.3
  2.6 0.0 copy-done.2
  2.6 0.3 fusion.1
  2.9 3.0 %collective-permute-start.1 = (bf16[2,512,768]{2,1,0:T(8,128)(2,1)S(1)}, bf16[2,512,768]{2,1,0:T(8,128)(2,1)S(1)}, u32[]{:S(2)}, u32[]{:S(2)}) collective-permute-start(bf16[2,512,768]{2,1,0:T(8,128)(2,1)S(1)} %bitcast.25), channel_id=1, source_target_pairs={{0,1},{1,2},{2,3},{3,4},{4,5},{5,6},{6,7},{7,8},{8,9},{9,10},{10,1... | collective-permute-start | bytes 4718600 | tf_op jit(solution)/shard_map/ppermute | solution.py:19
  5.9 3.5 %collective-permute-start.2 = (bf16[2,512,768]{2,1,0:T(8,128)(2,1)S(1)}, bf16[2,512,768]{2,1,0:T(8,128)(2,1)}, u32[]{:S(2)}, u32[]{:S(2)}) collective-permute-start(bf16[2,512,768]{2,1,0:T(8,128)(2,1)S(1)} %bitcast.26), channel_id=1, source_target_pairs={{0,31},{1,0},{2,1},{3,2},{4,3},{5,4},{6,5},{7,6},{8,7},{9,8},{10,9... | collective-permute-start | bytes 4718600 | tf_op jit(solution)/shard_map/ppermute | solution.py:19
  9.4 0.2 fusion.3
  9.6 0.7 fusion.2
  10.3 1.0 copy-done
  11.3 2.7 %fusion.15 = (f32[256,256]{1,0:T(8,128)S(1)}, f32[7,256,256]{2,1,0:T(8,128)}) fusion(f32[2,512,256]{2,1,0:T(8,128)S(1)} %bitcast.29), kind=kOutput, calls=%fused_computation.39 | convolution fusion | flops 805502976 | bytes 2883584 | tf_op jit(solution)/shard_map/lpr,lps->lrs/dot_general | solution.py:188
  14.0 0.1 collective-permute-start.4
  14.1 1.3 slice_bitcast_fusion
  15.3 0.0 collective-permute-start
  15.4 4.4 %collective-permute-start.3 = (bf16[1,512,768]{2,1,0:T(8,128)(2,1)}, bf16[1,512,768]{2,1,0:T(8,128)(2,1)}, u32[]{:S(2)}, u32[]{:S(2)}) collective-permute-start(bf16[1,512,768]{2,1,0:T(8,128)(2,1)} %get-tuple-element.10), channel_id=1, source_target_pairs={{0,30},{1,31},{2,0},{3,1},{4,2},{5,3},{6,4},{7,5},{8,6},{9,7},{10,... | collective-permute-start | bytes 2359304 | tf_op jit(solution)/shard_map/ppermute | solution.py:19
  19.8 0.7 bitcast_dynamic-update-slice_fusion.4
  20.5 67.0 %collective-permute-done.4 = f32[256,256]{1,0:T(8,128)S(1)} collective-permute-done((f32[256,256]{1,0:T(8,128)S(1)}, f32[256,256]{1,0:T(8,128)S(1)}, u32[]{:S(2)}, u32[]{:S(2)}) %collective-permute-start.4) | collective-permute-done | bytes 262176 | tf_op jit(solution)/shard_map/ppermute | solution.py:29
  87.5 0.7 bitcast_dynamic-update-slice_fusion.3
  88.3 0.8 bitcast_dynamic-update-slice_fusion.2
  89.1 0.3 collective-permute-start.5
  89.4 0.1 fusion.13.picks_ref
  89.5 7.0 %collective-permute-done.5 = f32[256,256]{1,0:T(8,128)S(1)} collective-permute-done((f32[256,256]{1,0:T(8,128)}, f32[256,256]{1,0:T(8,128)S(1)}, u32[]{:S(2)}, u32[]{:S(2)}) %collective-permute-start.5) | collective-permute-done | bytes 262176 | tf_op jit(solution)/shard_map/ppermute | solution.py:29
  96.5 0.7 bitcast_dynamic-update-slice_fusion.1
  97.2 1.7 %bitcast_dynamic-update-slice_fusion.grams_ref = f32[7,256,256]{2,1,0:T(8,128)} fusion(f32[7,256,256]{2,1,0:T(8,128)} %bitcast_dynamic-update-slice_fusion.1, f32[256,256]{1,0:T(8,128)} %get-tuple-element.9, f32[256,256]{1,0:T(8,128)S(1)} %collective-permute-done.5), kind=kLoop, calls=%fused_computation.22 | loop fusion | flops 131072 | bytes 786432 | tf_op jit(solution)/shard_map/stack | solution.py:196
  98.9 47.8 %factor.1 = (f32[7,256,256]{2,1,0:T(8,128)S(1)}, f32[7,256,256]{2,1,0:T(8,128)S(1)}) custom-call(f32[7,256,256]{2,1,0:T(8,128)} %bitcast_dynamic-update-slice_fusion.grams_ref), custom_call_target="tpu_custom_call" | custom-call | flops 40000000000 | bytes 8000000 | tf_op jit(solution)/shard_map/factor/pallas_call | solution.py:100
  146.7 1.5 convolution_bitcast_fusion.1
  148.2 1.5 convolution_bitcast_fusion
  149.6 1.9 %convolution_convert_fusion = bf16[2,512,256]{2,1,0:T(8,128)(2,1)} fusion(f32[2,512,256]{2,1,0:T(8,128)S(1)} %bitcast.30, f32[7,256,256]{2,1,0:T(8,128)S(1)} %get-tuple-element.6), kind=kOutput, calls=%fused_computation.6 | convolution fusion | flops 805568512 | bytes 2097152 | tf_op jit(solution)/shard_map/lpr,lsr->lps/dot_general | solution.py:197
  151.5 0.0 collective-permute-done.refs_0_
  151.5 0.0 collective-permute-done.3.refs_4_
  151.5 0.0 collective-permute-done.1.refs_1_
  151.6 0.0 collective-permute-done.2.refs_3_
  151.6 8.8 %near.1 = f32[1024,4,512]{2,1,0:T(4,128)} custom-call(s32[2,4]{1,0:T(2,128)S(1)} %fusion.13.picks_ref, bf16[1,512,768]{2,1,0:T(8,128)(2,1)} %collective-permute-done.refs_0_, bf16[2,512,768]{2,1,0:T(8,128)(2,1)S(1)} %collective-permute-done.1.refs_1_, bf16[2,512,768]{2,1,0:T(8,128)(2,1)S(1)} %bitcast.27, ...), custom_call_target="tpu_custom_call" | custom-call | flops 4000000000 | bytes 16000000 | tf_op jit(solution)/shard_map/near/pallas_call | solution.py:143
  (11 shorter events, 0.0 us)
Async XLA Ops:
  0.6 1.9 %copy-start.2 = (bf16[1024,768]{1,0:T(8,128)(2,1)S(1)}, bf16[1024,768]{1,0:T(8,128)(2,1)}, u32[]{:S(2)}) copy-start(bf16[1024,768]{1,0:T(8,128)(2,1)} %param.3) | copy-start | bytes 4718596
  2.5 6.9 %copy-start.3 = (bf16[256,768]{1,0:T(8,128)(2,1)S(1)}, bf16[256,768]{1,0:T(8,128)(2,1)}, u32[]{:S(2)}) copy-start(bf16[256,768]{1,0:T(8,128)(2,1)} %param.4) | copy-start | bytes 1179652
  2.9 148.6 %collective-permute-start.1 = (bf16[2,512,768]{2,1,0:T(8,128)(2,1)S(1)}, bf16[2,512,768]{2,1,0:T(8,128)(2,1)S(1)}, u32[]{:S(2)}, u32[]{:S(2)}) collective-permute-start(bf16[2,512,768]{2,1,0:T(8,128)(2,1)S(1)} %bitcast.25), channel_id=1, source_target_pairs={{0,1},{1,2},{2,3},{3,4},{4,5},{5,6},{6,7},{7,8},{8,9},{9,10},{10,1... | collective-permute-start | bytes 4718600 | tf_op jit(solution)/shard_map/ppermute | solution.py:19
  5.9 145.6 %collective-permute-start.2 = (bf16[2,512,768]{2,1,0:T(8,128)(2,1)S(1)}, bf16[2,512,768]{2,1,0:T(8,128)(2,1)}, u32[]{:S(2)}, u32[]{:S(2)}) collective-permute-start(bf16[2,512,768]{2,1,0:T(8,128)(2,1)S(1)} %bitcast.26), channel_id=1, source_target_pairs={{0,31},{1,0},{2,1},{3,2},{4,3},{5,4},{6,5},{7,6},{8,7},{9,8},{10,9... | collective-permute-start | bytes 4718600 | tf_op jit(solution)/shard_map/ppermute | solution.py:19
  10.3 1.0 copy-start
  14.0 73.6 %collective-permute-start.4 = (f32[256,256]{1,0:T(8,128)S(1)}, f32[256,256]{1,0:T(8,128)S(1)}, u32[]{:S(2)}, u32[]{:S(2)}) collective-permute-start(f32[256,256]{1,0:T(8,128)S(1)} %broadcast_multiply_fusion), channel_id=1, source_target_pairs={{0,1},{1,0},{2,3},{3,2},{4,5},{5,4},{6,7},{7,6},{8,9},{9,8},{10,11... | collective-permute-start | bytes 786440 | tf_op jit(solution)/shard_map/ppermute | solution.py:29
  15.3 74.1 %copy-start.4 = (s32[2,4]{1,0:T(2,128)S(1)}, s32[2,4]{1,0:T(2,128)}, u32[]{:S(2)}) copy-start(s32[2,4]{1,0:T(2,128)} %param.5) | copy-start | bytes 100
  15.3 136.2 %collective-permute-start = (bf16[1,512,768]{2,1,0:T(8,128)(2,1)}, bf16[1,512,768]{2,1,0:T(8,128)(2,1)}, u32[]{:S(2)}, u32[]{:S(2)}) collective-permute-start(bf16[1,512,768]{2,1,0:T(8,128)(2,1)} %get-tuple-element.11), channel_id=1, source_target_pairs={{0,2},{1,3},{2,4},{3,5},{4,6},{5,7},{6,8},{7,9},{8,10},{9,11},{10,... | collective-permute-start | bytes 2359304 | tf_op jit(solution)/shard_map/ppermute | solution.py:19
  15.4 136.2 %collective-permute-start.3 = (bf16[1,512,768]{2,1,0:T(8,128)(2,1)}, bf16[1,512,768]{2,1,0:T(8,128)(2,1)}, u32[]{:S(2)}, u32[]{:S(2)}) collective-permute-start(bf16[1,512,768]{2,1,0:T(8,128)(2,1)} %get-tuple-element.10), channel_id=1, source_target_pairs={{0,30},{1,31},{2,0},{3,1},{4,2},{5,3},{6,4},{7,5},{8,6},{9,7},{10,... | collective-permute-start | bytes 2359304 | tf_op jit(solution)/shard_map/ppermute | solution.py:19
  89.1 7.4 %collective-permute-start.5 = (f32[256,256]{1,0:T(8,128)}, f32[256,256]{1,0:T(8,128)S(1)}, u32[]{:S(2)}, u32[]{:S(2)}) collective-permute-start(f32[256,256]{1,0:T(8,128)} %get-tuple-element.9), channel_id=1, source_target_pairs={{0,2},{2,0},{1,3},{3,1},{4,6},{6,4},{5,7},{7,5},{8,10},{10,8},{9,1... | collective-permute-start | bytes 786440 | tf_op jit(solution)/shard_map/ppermute | solution.py:29
  146.7 2.9 %copy-start.1 = (f32[1024,256]{1,0:T(8,128)S(1)}, f32[1024,256]{1,0:T(8,128)}, u32[]{:S(2)}) copy-start(f32[1024,256]{1,0:T(8,128)} %copy-done) | copy-start | bytes 3145732

commit v2 on v1

--- a/solution.py
+++ b/solution.py
@@ -169,19 +169,15 @@
     anchor_unit = unit_rows(anchors)
     leaves = unit.reshape(leaves_dev, LEAF, width)
     reach = 3
-    lower_parts = []
-    upper_parts = []
     plan = []
     for step in range(1, (reach + leaves_dev - 1) // leaves_dev + 1):
         count = min(leaves_dev, reach - (step - 1) * leaves_dev)
         plan.append((leaves[leaves_dev - count :], step))
         plan.append((leaves[:count], -step))
+    got = {}
     for piece, step in plan:
-        got = from_behind(piece, ("group", "sub"), step)
-        if step > 0:
-            lower_parts.insert(0, got)
-        else:
-            upper_parts.append(got)
+        if abs(step) > 1:
+            got[step] = from_behind(piece, ("group", "sub"), step)
 
     sketch = jnp.exp(beta * jnp.dot(unit, anchor_unit.T, preferred_element_type=jnp.float32))
     sketch = sketch.reshape(leaves_dev, LEAF, rank)
@@ -193,6 +189,12 @@
         partner = from_partner(node, "sub", level)
         node = (node + partner) * 0.5
         stack += [partner, node]
+    near_pieces = [(piece, step) for piece, step in plan if abs(step) == 1]
+    held, stack = lax.optimization_barrier(([piece for piece, _ in near_pieces], stack))
+    for piece, (_, step) in zip(held, near_pieces):
+        got[step] = from_behind(piece, ("group", "sub"), step)
+    lower_parts = [got[step] for step in sorted(got, reverse=True) if step > 0]
+    upper_parts = [got[step] for step in sorted(got, reverse=True) if step < 0]
     upper, inverse = factors_of(jnp.stack(stack, axis=0))
     basis = jnp.einsum("lpr,lsr->lps", sketch, inverse[:leaves_dev], precision=HIGHEST)
     leaf_basis = basis.reshape(leaves_dev * LEAF, rank).astype(jnp.bfloat16)

time: 161 us -> 133 us (0.83)
  waiting for transfers between devices: 74 us -> 43.6 us
  Pallas kernels: 56.7 us -> 53.7 us
  starting transfers between devices: 11.4 us -> 13.9 us
  local copies, waits for them, and re-layouts: 3.71 us -> 5.97 us
    ppermute x2, waiting for transfers between devices: 74 us -> 34 us  [from_partner(): return lax.ppermute(block, axis, route)]
    ppermute x4, waiting for transfers between devices: 0.01 us -> 9.62 us  [from_behind(): return lax.ppermute(value, axis, pairs)]
    ppermute x2, starting transfers between devices: 0.41 us -> 4.78 us  [from_partner(): return lax.ppermute(block, axis, route)]
    ppermute x4, starting transfers between devices: 10.9 us -> 9.13 us  [from_behind(): return lax.ppermute(value, axis, pairs)]
    another operation x1 -> x0, other arithmetic: 1.69 us -> none  [shards(): upper, inverse = factors_of(jnp.stack(stack, axis=0))]
    unnamed x12 -> x16, local copies, waits for them, and re-layouts: 2.43 us -> 3.64 us
  transfers between devices with their start and end apart: 6 -> 6, of which waited for: 2 -> 3; matrix products, arithmetic and copies ran while one was open for 9% -> 8% of each run, Pallas kernels for 30% -> 35%
where the time goes in v2:
time: 133 us; the launch traced here: 131 us
  Pallas kernels  53.7 us (40%)
  waiting for transfers between devices  43.6 us (33%)
  starting transfers between devices  13.9 us (10%)
  matrix products  8.19 us (6%)
  local copies, waits for them, and re-layouts  5.97 us (4%)
  other arithmetic  5.21 us (4%)
    pallas_call x1, Pallas kernels, factors_of(): pl.pallas_call(functools.partial(factor_kernel, count, rank), out_shape=(...  46.3 us
    ppermute x2, waiting for transfers between devices, from_partner(): return lax.ppermute(block, axis, route)  34 us
    ppermute x4, waiting for transfers between devices, from_behind(): return lax.ppermute(value, axis, pairs)  9.62 us
    ppermute x4, starting transfers between devices, from_behind(): return lax.ppermute(value, axis, pairs)  9.13 us
    pallas_call x1, Pallas kernels, near_field(): pl.pallas_call(functools.partial(near_kernel, beta), out_shape=jax.ShapeD...  7.39 us
    ppermute x2, starting transfers between devices, from_partner(): return lax.ppermute(block, axis, route)  4.78 us
    unnamed x16, local copies, waits for them, and re-layouts  3.64 us
    reduce_sum x2, other arithmetic, unit_rows(): scale = lax.rsqrt(jnp.sum(wide * wide, axis=-1, keepdims=True) + 1e-06)  3.06 us
  transfers between devices with their start and end apart: 6, of which 3 were waited for; matrix products, arithmetic and copies ran while one was open for 8% of the time, Pallas kernels for 35%

profile of v2, /device:TPU:0, one launch (start us, length us, event | category | flops | bytes accessed | tf_op | source)
XLA Modules:
  0.0 131.4 jit_solution(1802973019591706232)
XLA Ops:
  0.6 0.0 copy-start.2
  0.6 1.3 fusion.3
  1.9 1.8 %fusion = f32[1024]{0:T(1024)S(1)} fusion(bf16[1024,768]{1,0:T(8,128)(2,1)} %param.3), kind=kLoop, calls=%fused_computation.2 | loop fusion | flops 2358272 | bytes 1576960 | tf_op jit(solution)/shard_map/reduce_sum | solution.py:34
  3.7 0.0 copy-start.3
  3.7 0.3 fusion.1
  4.1 0.6 copy-done.3
  4.7 0.7 fusion.2
  5.4 0.0 copy-start
  5.4 1.0 copy-done
  6.4 2.7 %fusion.15 = (f32[256,256]{1,0:T(8,128)S(1)}, f32[2,256,256]{2,1,0:T(8,128)}) fusion(f32[2,512,256]{2,1,0:T(8,128)S(1)} %bitcast.37), kind=kOutput, calls=%fused_computation.43 | convolution fusion | flops 805502976 | bytes 1835008 | tf_op jit(solution)/shard_map/lpr,lps->lrs/dot_general | solution.py:184
  9.1 0.7 broadcast_multiply_fusion
  9.8 2.9 %collective-permute-start.1 = (f32[256,256]{1,0:T(8,128)}, f32[256,256]{1,0:T(8,128)}, u32[]{:S(2)}, u32[]{:S(2)}) collective-permute-start(f32[256,256]{1,0:T(8,128)} %broadcast_multiply_fusion), channel_id=1, source_target_pairs={{0,1},{1,0},{2,3},{3,2},{4,5},{5,4},{6,7},{7,6},{8,9},{9,8},{10,11... | collective-permute-start | bytes 786440 | tf_op jit(solution)/shard_map/ppermute | solution.py:29
  12.7 1.3 slice_bitcast_fusion
  14.0 3.7 %collective-permute-start.5 = (bf16[1,512,768]{2,1,0:T(8,128)(2,1)}, bf16[1,512,768]{2,1,0:T(8,128)(2,1)S(1)}, u32[]{:S(2)}, u32[]{:S(2)}) collective-permute-start(bf16[1,512,768]{2,1,0:T(8,128)(2,1)} %get-tuple-element.26), channel_id=1, source_target_pairs={{0,30},{1,31},{2,0},{3,1},{4,2},{5,3},{6,4},{7,5},{8,6},{9,7},{10,... | collective-permute-start | bytes 2359304 | tf_op jit(solution)/shard_map/ppermute | solution.py:19
  17.7 0.0 collective-permute-start
  17.7 1.6 %collective-permute-done.1 = f32[256,256]{1,0:T(8,128)} collective-permute-done((f32[256,256]{1,0:T(8,128)}, f32[256,256]{1,0:T(8,128)}, u32[]{:S(2)}, u32[]{:S(2)}) %collective-permute-start.1) | collective-permute-done | bytes 262176 | tf_op jit(solution)/shard_map/ppermute | solution.py:29
  19.4 1.0 add_multiply_fusion.1
  20.3 1.8 %collective-permute-start.2 = (f32[256,256]{1,0:T(8,128)S(1)}, f32[256,256]{1,0:T(8,128)S(1)}, u32[]{:S(2)}, u32[]{:S(2)}) collective-permute-start(f32[256,256]{1,0:T(8,128)S(1)} %add_multiply_fusion.1), channel_id=1, source_target_pairs={{0,2},{2,0},{1,3},{3,1},{4,6},{6,4},{5,7},{7,5},{8,10},{10,8},{9,1... | collective-permute-start | bytes 786440 | tf_op jit(solution)/shard_map/ppermute | solution.py:29
  22.2 0.1 fusion.13.picks_ref
  22.3 1.1 slice_bitcast_fusion.2
  23.3 32.3 %collective-permute-done.2 = f32[256,256]{1,0:T(8,128)S(1)} collective-permute-done((f32[256,256]{1,0:T(8,128)S(1)}, f32[256,256]{1,0:T(8,128)S(1)}, u32[]{:S(2)}, u32[]{:S(2)}) %collective-permute-start.2) | collective-permute-done | bytes 262176 | tf_op jit(solution)/shard_map/ppermute | solution.py:29
  55.7 0.4 collective-permute-start.3
  56.1 5.0 %collective-permute-start.4 = (bf16[2,512,768]{2,1,0:T(8,128)(2,1)S(1)}, bf16[2,512,768]{2,1,0:T(8,128)(2,1)S(1)}, u32[]{:S(2)}, u32[]{:S(2)}) collective-permute-start(bf16[2,512,768]{2,1,0:T(8,128)(2,1)S(1)} %bitcast.34), channel_id=1, source_target_pairs={{0,31},{1,0},{2,1},{3,2},{4,3},{5,4},{6,5},{7,6},{8,7},{9,8},{10,9... | collective-permute-start | bytes 4718600 | tf_op jit(solution)/shard_map/ppermute | solution.py:19
  61.2 1.0 bitcast_dynamic-update-slice_fusion.4
  62.1 1.0 bitcast_dynamic-update-slice_fusion.3
  63.2 46.3 %factor.1 = (f32[7,256,256]{2,1,0:T(8,128)S(1)}, f32[7,256,256]{2,1,0:T(8,128)S(1)}) custom-call(f32[7,256,256]{2,1,0:T(8,128)S(1)} %bitcast_dynamic-update-slice_fusion.grams_ref), custom_call_target="tpu_custom_call" | custom-call | flops 40000000000 | bytes 8000000 | tf_op jit(solution)/shard_map/factor/pallas_call | solution.py:100
  109.5 0.0 copy-start.1
  109.5 1.5 %convolution_bitcast_fusion = f32[1,2,256,256]{3,2,1,0:T(8,128)} fusion(f32[7,256,256]{2,1,0:T(8,128)S(1)} %get-tuple-element.25, f32[7,256,256]{2,1,0:T(8,128)S(1)} %get-tuple-element.24), kind=kOutput, calls=%fused_computation.8 | convolution fusion | flops 402653184 | bytes 1572864 | tf_op jit(solution)/shard_map/tij,tkj->tik/dot_general | solution.py:205
  111.0 1.5 %convolution_bitcast_fusion.1 = f32[1,2,256,256]{3,2,1,0:T(8,128)} fusion(f32[7,256,256]{2,1,0:T(8,128)S(1)} %get-tuple-element.24, f32[7,256,256]{2,1,0:T(8,128)S(1)} %get-tuple-element.25), kind=kOutput, calls=%fused_computation.9 | convolution fusion | flops 402653184 | bytes 1572864 | tf_op jit(solution)/shard_map/tij,tkj->tik/dot_general | solution.py:204
  112.5 1.9 %convolution_convert_fusion = bf16[2,512,256]{2,1,0:T(8,128)(2,1)} fusion(f32[2,512,256]{2,1,0:T(8,128)S(1)} %bitcast.38, f32[7,256,256]{2,1,0:T(8,128)S(1)} %get-tuple-element.24), kind=kOutput, calls=%fused_computation.6 | convolution fusion | flops 805568512 | bytes 2097152 | tf_op jit(solution)/shard_map/lpr,lsr->lps/dot_general | solution.py:199
  114.4 9.6 %collective-permute-done.4.refs_3_ = bf16[2,512,768]{2,1,0:T(8,128)(2,1)S(1)} collective-permute-done((bf16[2,512,768]{2,1,0:T(8,128)(2,1)S(1)}, bf16[2,512,768]{2,1,0:T(8,128)(2,1)S(1)}, u32[]{:S(2)}, u32[]{:S(2)}) %collective-permute-start.4) | collective-permute-done | bytes 1572896 | tf_op jit(solution)/shard_map/ppermute | solution.py:19
  124.0 7.4 %near.1 = f32[1024,4,512]{2,1,0:T(4,128)} custom-call(s32[2,4]{1,0:T(2,128)S(1)} %fusion.13.picks_ref, bf16[1,512,768]{2,1,0:T(8,128)(2,1)S(1)} %collective-permute-done.refs_0_, bf16[2,512,768]{2,1,0:T(8,128)(2,1)S(1)} %collective-permute-done.3.refs_1_, bf16[2,512,768]{2,1,0:T(8,128)(2,1)S(1)} %bitcast.35, ...), custom_call_target="tpu_custom_call" | custom-call | flops 4000000000 | bytes 16000000 | tf_op jit(solution)/shard_map/near/pallas_call | solution.py:143
  (16 shorter events, 0.2 us)
Async XLA Ops:
  0.6 3.1 %copy-start.2 = (bf16[1024,768]{1,0:T(8,128)(2,1)S(1)}, bf16[1024,768]{1,0:T(8,128)(2,1)}, u32[]{:S(2)}) copy-start(bf16[1024,768]{1,0:T(8,128)(2,1)} %param.3) | copy-start | bytes 4718596
  3.7 1.0 copy-start.3
  5.4 1.0 copy-start
  9.8 12.4 %copy-start.4 = (s32[2,4]{1,0:T(2,128)S(1)}, s32[2,4]{1,0:T(2,128)}, u32[]{:S(2)}) copy-start(s32[2,4]{1,0:T(2,128)} %param.5) | copy-start | bytes 100
  9.8 9.6 %collective-permute-start.1 = (f32[256,256]{1,0:T(8,128)}, f32[256,256]{1,0:T(8,128)}, u32[]{:S(2)}, u32[]{:S(2)}) collective-permute-start(f32[256,256]{1,0:T(8,128)} %broadcast_multiply_fusion), channel_id=1, source_target_pairs={{0,1},{1,0},{2,3},{3,2},{4,5},{5,4},{6,7},{7,6},{8,9},{9,8},{10,11... | collective-permute-start | bytes 786440 | tf_op jit(solution)/shard_map/ppermute | solution.py:29
  14.0 100.4 %collective-permute-start.5 = (bf16[1,512,768]{2,1,0:T(8,128)(2,1)}, bf16[1,512,768]{2,1,0:T(8,128)(2,1)S(1)}, u32[]{:S(2)}, u32[]{:S(2)}) collective-permute-start(bf16[1,512,768]{2,1,0:T(8,128)(2,1)} %get-tuple-element.26), channel_id=1, source_target_pairs={{0,30},{1,31},{2,0},{3,1},{4,2},{5,3},{6,4},{7,5},{8,6},{9,7},{10,... | collective-permute-start | bytes 2359304 | tf_op jit(solution)/shard_map/ppermute | solution.py:19
  17.7 96.6 %collective-permute-start = (bf16[1,512,768]{2,1,0:T(8,128)(2,1)}, bf16[1,512,768]{2,1,0:T(8,128)(2,1)S(1)}, u32[]{:S(2)}, u32[]{:S(2)}) collective-permute-start(bf16[1,512,768]{2,1,0:T(8,128)(2,1)} %get-tuple-element.27), channel_id=1, source_target_pairs={{0,2},{1,3},{2,4},{3,5},{4,6},{5,7},{6,8},{7,9},{8,10},{9,11},{10,... | collective-permute-start | bytes 2359304 | tf_op jit(solution)/shard_map/ppermute | solution.py:19
  20.3 35.3 %collective-permute-start.2 = (f32[256,256]{1,0:T(8,128)S(1)}, f32[256,256]{1,0:T(8,128)S(1)}, u32[]{:S(2)}, u32[]{:S(2)}) collective-permute-start(f32[256,256]{1,0:T(8,128)S(1)} %add_multiply_fusion.1), channel_id=1, source_target_pairs={{0,2},{2,0},{1,3},{3,1},{4,6},{6,4},{5,7},{7,5},{8,10},{10,8},{9,1... | collective-permute-start | bytes 786440 | tf_op jit(solution)/shard_map/ppermute | solution.py:29
  55.7 58.7 %collective-permute-start.3 = (bf16[2,512,768]{2,1,0:T(8,128)(2,1)S(1)}, bf16[2,512,768]{2,1,0:T(8,128)(2,1)S(1)}, u32[]{:S(2)}, u32[]{:S(2)}) collective-permute-start(bf16[2,512,768]{2,1,0:T(8,128)(2,1)S(1)} %bitcast.33), channel_id=1, source_target_pairs={{0,1},{1,2},{2,3},{3,4},{4,5},{5,6},{6,7},{7,8},{8,9},{9,10},{10,1... | collective-permute-start | bytes 4718600 | tf_op jit(solution)/shard_map/ppermute | solution.py:19
  56.1 67.9 %collective-permute-start.4 = (bf16[2,512,768]{2,1,0:T(8,128)(2,1)S(1)}, bf16[2,512,768]{2,1,0:T(8,128)(2,1)S(1)}, u32[]{:S(2)}, u32[]{:S(2)}) collective-permute-start(bf16[2,512,768]{2,1,0:T(8,128)(2,1)S(1)} %bitcast.34), channel_id=1, source_target_pairs={{0,31},{1,0},{2,1},{3,2},{4,3},{5,4},{6,5},{7,6},{8,7},{9,8},{10,9... | collective-permute-start | bytes 4718600 | tf_op jit(solution)/shard_map/ppermute | solution.py:19
  109.5 2.9 %copy-start.1 = (f32[1024,256]{1,0:T(8,128)S(1)}, f32[1024,256]{1,0:T(8,128)}, u32[]{:S(2)}) copy-start(f32[1024,256]{1,0:T(8,128)} %copy-done) | copy-start | bytes 3145732

commit v3 on v2

--- a/solution.py
+++ b/solution.py
@@ -174,11 +174,6 @@
         count = min(leaves_dev, reach - (step - 1) * leaves_dev)
         plan.append((leaves[leaves_dev - count :], step))
         plan.append((leaves[:count], -step))
-    got = {}
-    for piece, step in plan:
-        if abs(step) > 1:
-            got[step] = from_behind(piece, ("group", "sub"), step)
-
     sketch = jnp.exp(beta * jnp.dot(unit, anchor_unit.T, preferred_element_type=jnp.float32))
     sketch = sketch.reshape(leaves_dev, LEAF, rank)
     grams = jnp.einsum("lpr,lps->lrs", sketch, sketch, precision=HIGHEST) / LEAF
@@ -189,10 +184,8 @@
         partner = from_partner(node, "sub", level)
         node = (node + partner) * 0.5
         stack += [partner, node]
-    near_pieces = [(piece, step) for piece, step in plan if abs(step) == 1]
-    held, stack = lax.optimization_barrier(([piece for piece, _ in near_pieces], stack))
-    for piece, (_, step) in zip(held, near_pieces):
-        got[step] = from_behind(piece, ("group", "sub"), step)
+    held, stack = lax.optimization_barrier(([piece for piece, _ in plan], stack))
+    got = {step: from_behind(piece, ("group", "sub"), step) for piece, (_, step) in zip(held, plan)}
     lower_parts = [got[step] for step in sorted(got, reverse=True) if step > 0]
     upper_parts = [got[step] for step in sorted(got, reverse=True) if step < 0]
     upper, inverse = factors_of(jnp.stack(stack, axis=0))

time: 133 us -> 115 us (0.86)
  waiting for transfers between devices: 43.6 us -> 30.1 us
  local copies, waits for them, and re-layouts: 5.97 us -> 2.82 us
    ppermute x2, waiting for transfers between devices: 34 us -> 12.1 us  [from_partner(): return lax.ppermute(block, axis, route)]
    ppermute x4, waiting for transfers between devices: 9.62 us -> 18 us  [from_behind(): return lax.ppermute(value, axis, pairs)]
    unnamed x16 -> x12, local copies, waits for them, and re-layouts: 3.64 us -> 2.67 us
  transfers between devices with their start and end apart: 6 -> 6, of which waited for: 3 -> 4; matrix products, arithmetic and copies ran while one was open for 8% -> 6% of each run, Pallas kernels for 35% -> 40%
where the time goes in v3:
time: 115 us
  Pallas kernels  53.7 us (47%)
  waiting for transfers between devices  30.1 us (26%)
  starting transfers between devices  14.6 us (13%)
  matrix products  7.36 us (6%)
  other arithmetic  5.21 us (5%)
  local copies, waits for them, and re-layouts  2.82 us (2%)
    pallas_call x1, Pallas kernels, factors_of(): pl.pallas_call(functools.partial(factor_kernel, count, rank), out_shape=(...  46.3 us
    ppermute x4, waiting for transfers between devices, from_behind(): return lax.ppermute(value, axis, pairs)  18 us
    ppermute x2, waiting for transfers between devices, from_partner(): return lax.ppermute(block, axis, route)  12.1 us
    ppermute x4, starting transfers between devices, from_behind(): return lax.ppermute(value, axis, pairs)  9.85 us
    pallas_call x1, Pallas kernels, near_field(): pl.pallas_call(functools.partial(near_kernel, beta), out_shape=jax.ShapeD...  7.39 us
    ppermute x2, starting transfers between devices, from_partner(): return lax.ppermute(block, axis, route)  4.79 us
    reduce_sum x2, other arithmetic, unit_rows(): scale = lax.rsqrt(jnp.sum(wide * wide, axis=-1, keepdims=True) + 1e-06)  3.06 us
    unnamed x12, local copies, waits for them, and re-layouts  2.67 us
  transfers between devices with their start and end apart: 6, of which 4 were waited for; matrix products, arithmetic and copies ran while one was open for 6% of the time, Pallas kernels for 40%

profile of v3, /device:TPU:0, one launch (start us, length us, event | category | flops | bytes accessed | tf_op | source)
XLA Modules:
  0.0 114.6 jit_solution(8201632471358495808)
XLA Ops:
  0.6 0.0 copy-start
  0.6 1.3 %fusion.3 = f32[256]{0:T(256)S(1)} fusion(bf16[256,768]{1,0:T(8,128)(2,1)} %param.4), kind=kLoop, calls=%fused_computation.12 | loop fusion | flops 589568 | bytes 394240 | tf_op jit(solution)/shard_map/reduce_sum | solution.py:34
  1.9 1.8 %fusion = f32[1024]{0:T(1024)S(1)} fusion(bf16[1024,768]{1,0:T(8,128)(2,1)} %param.3), kind=kLoop, calls=%fused_computation.2 | loop fusion | flops 2358272 | bytes 1576960 | tf_op jit(solution)/shard_map/reduce_sum | solution.py:34
  3.7 0.0 copy-start.1
  3.7 0.0 copy-done
  3.7 0.3 fusion.1
  4.1 0.6 copy-done.1
  4.7 0.7 fusion.2
  5.4 1.9 %fusion.15 = (f32[256,256]{1,0:T(8,128)S(1)}, f32[2,256,256]{2,1,0:T(8,128)S(1)}) fusion(f32[2,512,256]{2,1,0:T(8,128)S(1)} %bitcast.37), kind=kOutput, calls=%fused_computation.43 | convolution fusion | flops 805502976 | bytes 1835008 | tf_op jit(solution)/shard_map/lpr,lps->lrs/dot_general | solution.py:179
  7.3 0.7 broadcast_multiply_fusion
  8.0 2.9 %collective-permute-start = (f32[256,256]{1,0:T(8,128)}, f32[256,256]{1,0:T(8,128)}, u32[]{:S(2)}, u32[]{:S(2)}) collective-permute-start(f32[256,256]{1,0:T(8,128)} %broadcast_multiply_fusion), channel_id=1, source_target_pairs={{0,1},{1,0},{2,3},{3,2},{4,5},{5,4},{6,7},{7,6},{8,9},{9,8},{10,11... | collective-permute-start | bytes 786440 | tf_op jit(solution)/shard_map/ppermute | solution.py:29
  11.0 0.1 slice_bitcast_fusion
  11.1 6.5 %collective-permute-done = f32[256,256]{1,0:T(8,128)} collective-permute-done((f32[256,256]{1,0:T(8,128)}, f32[256,256]{1,0:T(8,128)}, u32[]{:S(2)}, u32[]{:S(2)}) %collective-permute-start) | collective-permute-done | bytes 262176 | tf_op jit(solution)/shard_map/ppermute | solution.py:29
  17.6 1.0 add_multiply_fusion.1
  18.6 1.8 %collective-permute-start.1 = (f32[256,256]{1,0:T(8,128)S(1)}, f32[256,256]{1,0:T(8,128)S(1)}, u32[]{:S(2)}, u32[]{:S(2)}) collective-permute-start(f32[256,256]{1,0:T(8,128)S(1)} %add_multiply_fusion.1), channel_id=1, source_target_pairs={{0,2},{2,0},{1,3},{3,1},{4,6},{6,4},{5,7},{7,5},{8,10},{10,8},{9,1... | collective-permute-start | bytes 786440 | tf_op jit(solution)/shard_map/ppermute | solution.py:29
  20.4 0.1 fusion.13.picks_ref
  20.5 5.6 %collective-permute-done.1 = f32[256,256]{1,0:T(8,128)S(1)} collective-permute-done((f32[256,256]{1,0:T(8,128)S(1)}, f32[256,256]{1,0:T(8,128)S(1)}, u32[]{:S(2)}, u32[]{:S(2)}) %collective-permute-start.1) | collective-permute-done | bytes 262176 | tf_op jit(solution)/shard_map/ppermute | solution.py:29
  26.2 1.5 %collective-permute-start.2 = (bf16[1,512,768]{2,1,0:T(8,128)(2,1)S(1)}, bf16[1,512,768]{2,1,0:T(8,128)(2,1)S(1)}, u32[]{:S(2)}, u32[]{:S(2)}) collective-permute-start(bf16[1,512,768]{2,1,0:T(8,128)(2,1)S(1)} %get-tuple-element.17), channel_id=1, source_target_pairs={{0,2},{1,3},{2,4},{3,5},{4,6},{5,7},{6,8},{7,9},{8,10},{9,11},{10,... | collective-permute-start | bytes 2359304 | tf_op jit(solution)/shard_map/ppermute | solution.py:19
  27.7 3.0 %collective-permute-start.5 = (bf16[1,512,768]{2,1,0:T(8,128)(2,1)S(1)}, bf16[1,512,768]{2,1,0:T(8,128)(2,1)S(1)}, u32[]{:S(2)}, u32[]{:S(2)}) collective-permute-start(bf16[1,512,768]{2,1,0:T(8,128)(2,1)S(1)} %get-tuple-element.20), channel_id=1, source_target_pairs={{0,30},{1,31},{2,0},{3,1},{4,2},{5,3},{6,4},{7,5},{8,6},{9,7},{10,... | collective-permute-start | bytes 2359304 | tf_op jit(solution)/shard_map/ppermute | solution.py:19
  30.7 1.4 %collective-permute-start.3 = (bf16[2,512,768]{2,1,0:T(8,128)(2,1)S(1)}, bf16[2,512,768]{2,1,0:T(8,128)(2,1)S(1)}, u32[]{:S(2)}, u32[]{:S(2)}) collective-permute-start(bf16[2,512,768]{2,1,0:T(8,128)(2,1)S(1)} %bitcast.33), channel_id=1, source_target_pairs={{0,1},{1,2},{2,3},{3,4},{4,5},{5,6},{6,7},{7,8},{8,9},{9,10},{10,1... | collective-permute-start | bytes 4718600 | tf_op jit(solution)/shard_map/ppermute | solution.py:19
  32.1 3.9 %collective-permute-start.4 = (bf16[2,512,768]{2,1,0:T(8,128)(2,1)S(1)}, bf16[2,512,768]{2,1,0:T(8,128)(2,1)S(1)}, u32[]{:S(2)}, u32[]{:S(2)}) collective-permute-start(bf16[2,512,768]{2,1,0:T(8,128)(2,1)S(1)} %bitcast.34), channel_id=1, source_target_pairs={{0,31},{1,0},{2,1},{3,2},{4,3},{5,4},{6,5},{7,6},{8,7},{9,8},{10,9... | collective-permute-start | bytes 4718600 | tf_op jit(solution)/shard_map/ppermute | solution.py:19
  36.0 1.0 bitcast_dynamic-update-slice_fusion.4
  37.0 1.0 bitcast_dynamic-update-slice_fusion.3
  38.1 46.3 %factor.1 = (f32[7,256,256]{2,1,0:T(8,128)S(1)}, f32[7,256,256]{2,1,0:T(8,128)S(1)}) custom-call(f32[7,256,256]{2,1,0:T(8,128)S(1)} %bitcast_dynamic-update-slice_fusion.grams_ref), custom_call_target="tpu_custom_call" | custom-call | flops 40000000000 | bytes 8000000 | tf_op jit(solution)/shard_map/factor/pallas_call | solution.py:100
  84.4 1.5 %convolution_bitcast_fusion = f32[1,2,256,256]{3,2,1,0:T(8,128)} fusion(f32[7,256,256]{2,1,0:T(8,128)S(1)} %get-tuple-element.29, f32[7,256,256]{2,1,0:T(8,128)S(1)} %get-tuple-element.28), kind=kOutput, calls=%fused_computation.8 | convolution fusion | flops 402653184 | bytes 1572864 | tf_op jit(solution)/shard_map/tij,tkj->tik/dot_general | solution.py:198
  85.9 1.5 %convolution_bitcast_fusion.1 = f32[1,2,256,256]{3,2,1,0:T(8,128)} fusion(f32[7,256,256]{2,1,0:T(8,128)S(1)} %get-tuple-element.28, f32[7,256,256]{2,1,0:T(8,128)S(1)} %get-tuple-element.29), kind=kOutput, calls=%fused_computation.9 | convolution fusion | flops 402653184 | bytes 1572864 | tf_op jit(solution)/shard_map/tij,tkj->tik/dot_general | solution.py:197
  87.3 1.9 %convolution_convert_fusion = bf16[2,512,256]{2,1,0:T(8,128)(2,1)} fusion(f32[2,512,256]{2,1,0:T(8,128)S(1)} %bitcast.38, f32[7,256,256]{2,1,0:T(8,128)S(1)} %get-tuple-element.28), kind=kOutput, calls=%fused_computation.6 | convolution fusion | flops 805568512 | bytes 2097152 | tf_op jit(solution)/shard_map/lpr,lsr->lps/dot_general | solution.py:192
  89.2 0.0 collective-permute-done.2.refs_0_
  89.2 7.4 %collective-permute-done.5.refs_4_ = bf16[1,512,768]{2,1,0:T(8,128)(2,1)S(1)} collective-permute-done((bf16[1,512,768]{2,1,0:T(8,128)(2,1)S(1)}, bf16[1,512,768]{2,1,0:T(8,128)(2,1)S(1)}, u32[]{:S(2)}, u32[]{:S(2)}) %collective-permute-start.5) | collective-permute-done | bytes 786464 | tf_op jit(solution)/shard_map/ppermute | solution.py:19
  96.6 0.0 collective-permute-done.3.refs_1_
  96.6 10.6 %collective-permute-done.4.refs_3_ = bf16[2,512,768]{2,1,0:T(8,128)(2,1)S(1)} collective-permute-done((bf16[2,512,768]{2,1,0:T(8,128)(2,1)S(1)}, bf16[2,512,768]{2,1,0:T(8,128)(2,1)S(1)}, u32[]{:S(2)}, u32[]{:S(2)}) %collective-permute-start.4) | collective-permute-done | bytes 1572896 | tf_op jit(solution)/shard_map/ppermute | solution.py:19
  107.2 7.4 %near.1 = f32[1024,4,512]{2,1,0:T(4,128)} custom-call(s32[2,4]{1,0:T(2,128)S(1)} %fusion.13.picks_ref, bf16[1,512,768]{2,1,0:T(8,128)(2,1)S(1)} %collective-permute-done.2.refs_0_, bf16[2,512,768]{2,1,0:T(8,128)(2,1)S(1)} %collective-permute-done.3.refs_1_, bf16[2,512,768]{2,1,0:T(8,128)(2,1)S(1)} %bitcast.35, ...), custom_call_target="tpu_custom_call" | custom-call | flops 4000000000 | bytes 16000000 | tf_op jit(solution)/shard_map/near/pallas_call | solution.py:143
  (12 shorter events, 0.2 us)
Async XLA Ops:
  0.6 3.1 %copy-start = (bf16[1024,768]{1,0:T(8,128)(2,1)S(1)}, bf16[1024,768]{1,0:T(8,128)(2,1)}, u32[]{:S(2)}) copy-start(bf16[1024,768]{1,0:T(8,128)(2,1)} %param.3) | copy-start | bytes 4718596
  3.7 1.0 copy-start.1
  8.0 9.6 %collective-permute-start = (f32[256,256]{1,0:T(8,128)}, f32[256,256]{1,0:T(8,128)}, u32[]{:S(2)}, u32[]{:S(2)}) collective-permute-start(f32[256,256]{1,0:T(8,128)} %broadcast_multiply_fusion), channel_id=1, source_target_pairs={{0,1},{1,0},{2,3},{3,2},{4,5},{5,4},{6,7},{7,6},{8,9},{9,8},{10,11... | collective-permute-start | bytes 786440 | tf_op jit(solution)/shard_map/ppermute | solution.py:29
  11.0 9.4 %copy-start.2 = (s32[2,4]{1,0:T(2,128)S(1)}, s32[2,4]{1,0:T(2,128)}, u32[]{:S(2)}) copy-start(s32[2,4]{1,0:T(2,128)} %param.5) | copy-start | bytes 100
  18.6 7.6 %collective-permute-start.1 = (f32[256,256]{1,0:T(8,128)S(1)}, f32[256,256]{1,0:T(8,128)S(1)}, u32[]{:S(2)}, u32[]{:S(2)}) collective-permute-start(f32[256,256]{1,0:T(8,128)S(1)} %add_multiply_fusion.1), channel_id=1, source_target_pairs={{0,2},{2,0},{1,3},{3,1},{4,6},{6,4},{5,7},{7,5},{8,10},{10,8},{9,1... | collective-permute-start | bytes 786440 | tf_op jit(solution)/shard_map/ppermute | solution.py:29
  26.2 63.1 %collective-permute-start.2 = (bf16[1,512,768]{2,1,0:T(8,128)(2,1)S(1)}, bf16[1,512,768]{2,1,0:T(8,128)(2,1)S(1)}, u32[]{:S(2)}, u32[]{:S(2)}) collective-permute-start(bf16[1,512,768]{2,1,0:T(8,128)(2,1)S(1)} %get-tuple-element.17), channel_id=1, source_target_pairs={{0,2},{1,3},{2,4},{3,5},{4,6},{5,7},{6,8},{7,9},{8,10},{9,11},{10,... | collective-permute-start | bytes 2359304 | tf_op jit(solution)/shard_map/ppermute | solution.py:19
  27.7 69.0 %collective-permute-start.5 = (bf16[1,512,768]{2,1,0:T(8,128)(2,1)S(1)}, bf16[1,512,768]{2,1,0:T(8,128)(2,1)S(1)}, u32[]{:S(2)}, u32[]{:S(2)}) collective-permute-start(bf16[1,512,768]{2,1,0:T(8,128)(2,1)S(1)} %get-tuple-element.20), channel_id=1, source_target_pairs={{0,30},{1,31},{2,0},{3,1},{4,2},{5,3},{6,4},{7,5},{8,6},{9,7},{10,... | collective-permute-start | bytes 2359304 | tf_op jit(solution)/shard_map/ppermute | solution.py:19
  30.7 66.0 %collective-permute-start.3 = (bf16[2,512,768]{2,1,0:T(8,128)(2,1)S(1)}, bf16[2,512,768]{2,1,0:T(8,128)(2,1)S(1)}, u32[]{:S(2)}, u32[]{:S(2)}) collective-permute-start(bf16[2,512,768]{2,1,0:T(8,128)(2,1)S(1)} %bitcast.33), channel_id=1, source_target_pairs={{0,1},{1,2},{2,3},{3,4},{4,5},{5,6},{6,7},{7,8},{8,9},{9,10},{10,1... | collective-permute-start | bytes 4718600 | tf_op jit(solution)/shard_map/ppermute | solution.py:19
  32.1 75.1 %collective-permute-start.4 = (bf16[2,512,768]{2,1,0:T(8,128)(2,1)S(1)}, bf16[2,512,768]{2,1,0:T(8,128)(2,1)S(1)}, u32[]{:S(2)}, u32[]{:S(2)}) collective-permute-start(bf16[2,512,768]{2,1,0:T(8,128)(2,1)S(1)} %bitcast.34), channel_id=1, source_target_pairs={{0,31},{1,0},{2,1},{3,2},{4,3},{5,4},{6,5},{7,6},{8,7},{9,8},{10,9... | collective-permute-start | bytes 4718600 | tf_op jit(solution)/shard_map/ppermute | solution.py:19

commit v4 on v3

--- a/solution.py
+++ b/solution.py
@@ -17,16 +17,6 @@
     count = lax.axis_size(axis)
     pairs = [(source, (source + steps) % count) for source in range(count)]
     return lax.ppermute(value, axis, pairs)
-
-
-def from_partner(block, axis, stride):
-    count = lax.axis_size(axis)
-    route = []
-    for low in range(count):
-        high = low | 1 << stride
-        if high != low and high < count:
-            route += [(low, high), (high, low)]
-    return lax.ppermute(block, axis, route)
 
 
 def unit_rows(values):
@@ -174,18 +164,19 @@
         count = min(leaves_dev, reach - (step - 1) * leaves_dev)
         plan.append((leaves[leaves_dev - count :], step))
         plan.append((leaves[:count], -step))
+    got = {step: from_behind(piece, ("group", "sub"), step) for piece, step in plan}
     sketch = jnp.exp(beta * jnp.dot(unit, anchor_unit.T, preferred_element_type=jnp.float32))
     sketch = sketch.reshape(leaves_dev, LEAF, rank)
     grams = jnp.einsum("lpr,lps->lrs", sketch, sketch, precision=HIGHEST) / LEAF
     node = jnp.sum(grams, axis=0) / leaves_dev
     levels = lax.axis_size("sub").bit_length() - 1
+    mine = lax.axis_index("sub")
     stack = [grams[leaf] for leaf in range(leaves_dev)] + [node]
+    nodes = lax.all_gather(node, "sub", axis=0)
     for level in range(levels):
-        partner = from_partner(node, "sub", level)
-        node = (node + partner) * 0.5
-        stack += [partner, node]
-    held, stack = lax.optimization_barrier(([piece for piece, _ in plan], stack))
-    got = {step: from_behind(piece, ("group", "sub"), step) for piece, (_, step) in zip(held, plan)}
+        stack.append(lax.dynamic_index_in_dim(nodes, (mine >> level) ^ 1, 0, keepdims=False))
+        nodes = (nodes[0::2] + nodes[1::2]) * 0.5
+        stack.append(lax.dynamic_index_in_dim(nodes, mine >> (level + 1), 0, keepdims=False))
     lower_parts = [got[step] for step in sorted(got, reverse=True) if step > 0]
     upper_parts = [got[step] for step in sorted(got, reverse=True) if step < 0]
     upper, inverse = factors_of(jnp.stack(stack, axis=0))

time: 115 us -> 171 us (1.49)
  the two profiles are of different devices: /device:TPU:0 before, /device:TPU:11 now
where the time goes in v4:
time: 171 us
  waiting for transfers between devices  76.8 us (45%)
  Pallas kernels  55.2 us (32%)
  between operations  14.2 us (8%)
  matrix products  8.19 us (5%)
  local copies, waits for them, and re-layouts  6.59 us (4%)
  other arithmetic  5.9 us (3%)
  starting transfers between devices  3.96 us (2%)
    all_gather x1, waiting for transfers between devices, shards(): nodes = lax.all_gather(node, 'sub', axis=0)  76.8 us
    pallas_call x1, Pallas kernels, factors_of(): pl.pallas_call(functools.partial(factor_kernel, count, rank), out_shape=(...  46.3 us
    pallas_call x1, Pallas kernels, near_field(): pl.pallas_call(functools.partial(near_kernel, beta), out_shape=jax.ShapeD...  8.85 us
    unnamed x15, local copies, waits for them, and re-layouts  5.27 us
    ppermute x4, starting transfers between devices, from_behind(): return lax.ppermute(value, axis, pairs)  3.92 us
  transfers between devices with their start and end apart: 5, of which 1 were waited for; matrix products, arithmetic and copies ran while one was open for 7% of the time, Pallas kernels for 27%

profile of v4, /device:TPU:11, one launch (start us, length us, event | category | flops | bytes accessed | tf_op | source)
XLA Modules:
  0.0 170.8 jit_solution(13356488734066553479)
XLA Ops:
  7.2 0.0 all-gather.3.cloned.1.call-start
  7.2 1.9 %fusion = f32[1024]{0:T(1024)S(1)} fusion(bf16[1024,768]{1,0:T(8,128)(2,1)} %param.3), kind=kLoop, calls=%fused_computation.2 | loop fusion | flops 2358272 | bytes 1576960 | tf_op jit(solution)/shard_map/reduce_sum | solution.py:24
  9.1 0.0 copy-start.4
  9.2 0.3 fusion.1
  9.5 0.6 copy-done.4
  10.1 0.2 fusion.3
  10.3 0.7 fusion.2
  11.0 2.7 %fusion.17 = (f32[256,256]{1,0:T(8,128)S(1)}, f32[7,256,256]{2,1,0:T(8,128)}) fusion(f32[2,512,256]{2,1,0:T(8,128)S(1)} %bitcast.22), kind=kOutput, calls=%fused_computation.41 | convolution fusion | flops 805502976 | bytes 2883584 | tf_op jit(solution)/shard_map/lpr,lps->lrs/dot_general | solution.py:170
  13.7 0.7 broadcast_multiply_fusion
  14.4 0.0 all-gather.3.cloned.1.call-update
  14.4 1.3 collective-permute-start.1
  15.7 0.3 collective-permute-start.2
  16.0 1.3 slice_bitcast_fusion
  17.3 1.6 collective-permute-start
  18.8 0.8 collective-permute-start.3
  19.7 0.1 fusion.15.picks_ref
  19.8 0.7 bitcast_dynamic-update-slice_fusion
  20.5 76.8 %all-gather.3.cloned.1.call-done = f32[1024,256]{1,0:T(8,128)} async-done(((f32[256,256]{1,0:T(8,128)}), f32[1024,256]{1,0:T(8,128)}) %all-gather.3.cloned.1.call-update) | async-done | bytes 1048592 | tf_op jit(solution)/shard_map/all_gather | solution.py:175
  97.3 1.3 add_multiply_fusion
  98.5 1.7 dynamic-slice_dynamic-update-slice_fusion.2
  100.2 0.7 dynamic-slice_dynamic-update-slice_fusion.1
  100.9 0.7 dynamic-slice_dynamic-update-slice_fusion
  101.6 0.7 fusion.13.grams_ref
  102.4 1.5 copy-done
  103.9 46.3 %factor.1 = (f32[7,256,256]{2,1,0:T(8,128)S(1)}, f32[7,256,256]{2,1,0:T(8,128)S(1)}) custom-call(f32[7,256,256]{2,1,0:T(8,128)S(1)} %copy-done), custom_call_target="tpu_custom_call" | custom-call | flops 40000000000 | bytes 8000000 | tf_op jit(solution)/shard_map/factor/pallas_call | solution.py:90
  150.2 1.5 convolution_bitcast_fusion.1
  151.7 1.5 convolution_bitcast_fusion
  153.2 1.9 %convolution_convert_fusion = bf16[2,512,256]{2,1,0:T(8,128)(2,1)} fusion(f32[2,512,256]{2,1,0:T(8,128)S(1)} %bitcast.23, f32[7,256,256]{2,1,0:T(8,128)S(1)} %get-tuple-element.6), kind=kOutput, calls=%fused_computation.6 | convolution fusion | flops 805568512 | bytes 2097152 | tf_op jit(solution)/shard_map/lpr,lsr->lps/dot_general | solution.py:183
  155.0 0.0 collective-permute-done.refs_0_
  155.0 0.0 collective-permute-done.3.refs_4_
  155.1 0.0 collective-permute-done.1.refs_1_
  155.1 8.8 %near.1 = f32[1024,4,512]{2,1,0:T(4,128)} custom-call(s32[2,4]{1,0:T(2,128)S(1)} %fusion.15.picks_ref, bf16[1,512,768]{2,1,0:T(8,128)(2,1)} %collective-permute-done.refs_0_, bf16[2,512,768]{2,1,0:T(8,128)(2,1)S(1)} %collective-permute-done.1.refs_1_, bf16[2,512,768]{2,1,0:T(8,128)(2,1)S(1)} %bitcast.20, ...), custom_call_target="tpu_custom_call" | custom-call | flops 4000000000 | bytes 16000000 | tf_op jit(solution)/shard_map/near/pallas_call | solution.py:133
  (13 shorter events, 0.0 us)
Async XLA Ops:
  7.2 2.0 %copy-start.3 = (bf16[1024,768]{1,0:T(8,128)(2,1)S(1)}, bf16[1024,768]{1,0:T(8,128)(2,1)}, u32[]{:S(2)}) copy-start(bf16[1024,768]{1,0:T(8,128)(2,1)} %param.3) | copy-start | bytes 4718596
  7.2 90.1 %all-gather.3.cloned.1.call-start = ((), (), s32[]{:S(2)}) async-start(), calls=%async_computation | async-start | bytes 1310720 | tf_op jit(solution)/shard_map/all_gather | solution.py:175
  9.1 1.0 copy-start.4
  11.0 3.5 %copy-start.1 = (f32[1024,256]{1,0:T(8,128)}, f32[1024,256]{1,0:T(8,128)S(1)}, u32[]{:S(2)}) copy-start(f32[1024,256]{1,0:T(8,128)S(1)} %fusion.2) | copy-start | bytes 3145732
  14.4 5.3 %copy-start.5 = (s32[2,4]{1,0:T(2,128)S(1)}, s32[2,4]{1,0:T(2,128)}, u32[]{:S(2)}) copy-start(s32[2,4]{1,0:T(2,128)} %param.5) | copy-start | bytes 100
  14.4 140.6 %collective-permute-start.1 = (bf16[2,512,768]{2,1,0:T(8,128)(2,1)S(1)}, bf16[2,512,768]{2,1,0:T(8,128)(2,1)S(1)}, u32[]{:S(2)}, u32[]{:S(2)}) collective-permute-start(bf16[2,512,768]{2,1,0:T(8,128)(2,1)S(1)} %bitcast.18), channel_id=1, source_target_pairs={{0,1},{1,2},{2,3},{3,4},{4,5},{5,6},{6,7},{7,8},{8,9},{9,10},{10,1... | collective-permute-start | bytes 4718600 | tf_op jit(solution)/shard_map/ppermute | solution.py:19
  15.7 139.3 %collective-permute-start.2 = (bf16[2,512,768]{2,1,0:T(8,128)(2,1)S(1)}, bf16[2,512,768]{2,1,0:T(8,128)(2,1)}, u32[]{:S(2)}, u32[]{:S(2)}) collective-permute-start(bf16[2,512,768]{2,1,0:T(8,128)(2,1)S(1)} %bitcast.19), channel_id=1, source_target_pairs={{0,31},{1,0},{2,1},{3,2},{4,3},{5,4},{6,5},{7,6},{8,7},{9,8},{10,9... | collective-permute-start | bytes 4718600 | tf_op jit(solution)/shard_map/ppermute | solution.py:19
  17.3 137.8 %collective-permute-start = (bf16[1,512,768]{2,1,0:T(8,128)(2,1)}, bf16[1,512,768]{2,1,0:T(8,128)(2,1)}, u32[]{:S(2)}, u32[]{:S(2)}) collective-permute-start(bf16[1,512,768]{2,1,0:T(8,128)(2,1)} %get-tuple-element.9), channel_id=1, source_target_pairs={{0,2},{1,3},{2,4},{3,5},{4,6},{5,7},{6,8},{7,9},{8,10},{9,11},{10,... | collective-permute-start | bytes 2359304 | tf_op jit(solution)/shard_map/ppermute | solution.py:19
  18.8 136.2 %collective-permute-start.3 = (bf16[1,512,768]{2,1,0:T(8,128)(2,1)}, bf16[1,512,768]{2,1,0:T(8,128)(2,1)}, u32[]{:S(2)}, u32[]{:S(2)}) collective-permute-start(bf16[1,512,768]{2,1,0:T(8,128)(2,1)} %get-tuple-element.8), channel_id=1, source_target_pairs={{0,30},{1,31},{2,0},{3,1},{4,2},{5,3},{6,4},{7,5},{8,6},{9,7},{10,... | collective-permute-start | bytes 2359304 | tf_op jit(solution)/shard_map/ppermute | solution.py:19
  102.4 1.5 copy-start
  150.2 2.9 %copy-start.2 = (f32[1024,256]{1,0:T(8,128)S(1)}, f32[1024,256]{1,0:T(8,128)}, u32[]{:S(2)}) copy-start(f32[1024,256]{1,0:T(8,128)} %copy-done.1) | copy-start | bytes 3145732
Sparse Core Ops, SparseCore 0:
  14.6 82.6 all-gather.2

commit v5 on v3

--- a/solution.py
+++ b/solution.py
@@ -129,7 +129,7 @@
 
     rows = rows_ref[0]
     for j in range(out_ref.shape[1]):
-        cols = window[picks_ref[leaf, j]]
+        cols = window[pl.ds(pl.multiple_of(picks_ref[leaf, j] * LEAF, LEAF), LEAF), :]
         scores = lax.dot_general(rows, cols, (((1,), (1,)), ((), ())), preferred_element_type=jnp.float32)
         out_ref[:, j, :] = jnp.exp(beta * scores)
 
@@ -150,7 +150,7 @@
             + [pl.BlockSpec((1, chunk, width), lambda a, c, p: (a, c, 0))],
             out_specs=pl.BlockSpec((chunk, nbr, leaf), lambda a, c, p: (a * steps + c, 0, 0)),
             scratch_shapes=[
-                pltpu.VMEM((total, leaf, width), jnp.bfloat16),
+                pltpu.VMEM((total, width), jnp.bfloat16),
                 pltpu.SemaphoreType.DMA((len(parts),)),
             ],
         ),
@@ -174,6 +174,15 @@
         count = min(leaves_dev, reach - (step - 1) * leaves_dev)
         plan.append((leaves[leaves_dev - count :], step))
         plan.append((leaves[:count], -step))
+    share = LEAF // 2
+    first = {}
+    late = []
+    for piece, step in plan:
+        piece = piece.reshape(-1, width)
+        if abs(step) == 1:
+            first[step] = from_behind(piece[:share], ("group", "sub"), step)
+            piece = piece[share:]
+        late.append((piece, step))
     sketch = jnp.exp(beta * jnp.dot(unit, anchor_unit.T, preferred_element_type=jnp.float32))
     sketch = sketch.reshape(leaves_dev, LEAF, rank)
     grams = jnp.einsum("lpr,lps->lrs", sketch, sketch, precision=HIGHEST) / LEAF
@@ -184,10 +193,12 @@
         partner = from_partner(node, "sub", level)
         node = (node + partner) * 0.5
         stack += [partner, node]
-    held, stack = lax.optimization_barrier(([piece for piece, _ in plan], stack))
-    got = {step: from_behind(piece, ("group", "sub"), step) for piece, (_, step) in zip(held, plan)}
-    lower_parts = [got[step] for step in sorted(got, reverse=True) if step > 0]
-    upper_parts = [got[step] for step in sorted(got, reverse=True) if step < 0]
+    held, stack, first = lax.optimization_barrier(([piece for piece, _ in late], stack, first))
+    got = {step: [from_behind(piece, ("group", "sub"), step)] for piece, (_, step) in zip(held, late)}
+    for step, piece in first.items():
+        got[step].insert(0, piece)
+    lower_parts = [piece for step in sorted(got, reverse=True) if step > 0 for piece in got[step]]
+    upper_parts = [piece for step in sorted(got, reverse=True) if step < 0 for piece in got[step]]
     upper, inverse = factors_of(jnp.stack(stack, axis=0))
     basis = jnp.einsum("lpr,lsr->lps", sketch, inverse[:leaves_dev], precision=HIGHEST)
     leaf_basis = basis.reshape(leaves_dev * LEAF, rank).astype(jnp.bfloat16)
@@ -202,7 +213,7 @@
     local = jnp.arange(leaves_dev, dtype=jnp.int32)[:, None]
     offsets = jnp.remainder(neighbours - first_leaf - local + reach, total_leaves) - reach
     picks = reach + local + offsets
-    near_blocks = near_field(lower_parts + [leaves] + upper_parts, leaves, picks, beta)
+    near_blocks = near_field(lower_parts + [unit] + upper_parts, leaves, picks, beta)
     return (near_blocks, leaf_basis, transfer, coupling)
 
 

time: 115 us -> 114 us (level)
  waiting for transfers between devices: 30.1 us -> 21.3 us
  local copies, waits for them, and re-layouts: 2.82 us -> 7.9 us
  starting transfers between devices: 14.6 us -> 17.5 us
    ppermute x4 -> x6, waiting for transfers between devices: 18 us -> 0.02 us  [from_behind(): return lax.ppermute(value, axis, pairs)]
    ppermute x2, waiting for transfers between devices: 12.1 us -> 21.3 us  [from_partner(): return lax.ppermute(block, axis, route)]
    ppermute x4 -> x6, starting transfers between devices: 9.85 us -> 16.2 us  [from_behind(): return lax.ppermute(value, axis, pairs)]
    ppermute x2, starting transfers between devices: 4.79 us -> 1.24 us  [from_partner(): return lax.ppermute(block, axis, route)]
    slice x0 -> x2, local copies, waits for them, and re-layouts: none -> 1.86 us  [the longest x1 1.09 us: shards(): piece = piece[share:]]
    unnamed x12 -> x20, local copies, waits for them, and re-layouts: 2.67 us -> 3.94 us
    slice x1, local copies, waits for them, and re-layouts: 0.1 us -> 1.25 us  [shards(): plan.append((leaves[:count], -step))]
  transfers between devices with their start and end apart: 6 -> 8, of which waited for: 4 -> 2; matrix products, arithmetic and copies ran while one was open for 6% -> 15% of each run, Pallas kernels for 40% -> 41%
where the time goes in v5:
time: 114 us
  Pallas kernels  54.4 us (48%)
  waiting for transfers between devices  21.3 us (19%)
  starting transfers between devices  17.5 us (15%)
  local copies, waits for them, and re-layouts  7.9 us (7%)
  matrix products  7.39 us (6%)
  other arithmetic  4.34 us (4%)
    pallas_call x1, Pallas kernels, factors_of(): pl.pallas_call(functools.partial(factor_kernel, count, rank), out_shape=(...  46.3 us
    ppermute x2, waiting for transfers between devices, from_partner(): return lax.ppermute(block, axis, route)  21.3 us
    ppermute x6, starting transfers between devices, from_behind(): return lax.ppermute(value, axis, pairs)  16.2 us
    pallas_call x1, Pallas kernels, near_field(): pl.pallas_call(functools.partial(near_kernel, beta), out_shape=jax.ShapeD...  8.06 us
    unnamed x20, local copies, waits for them, and re-layouts  3.94 us
  transfers between devices with their start and end apart: 8, of which 2 were waited for; matrix products, arithmetic and copies ran while one was open for 15% of the time, Pallas kernels for 41%

profile of v5, /device:TPU:0, one launch (start us, length us, event | category | flops | bytes accessed | tf_op | source)
XLA Modules:
  0.0 113.6 jit_solution(4720904113329757114)
XLA Ops:
  0.6 1.9 %fusion = f32[1024]{0:T(1024)S(1)} fusion(bf16[1024,768]{1,0:T(8,128)(2,1)} %param.3), kind=kLoop, calls=%fused_computation.2 | loop fusion | flops 2358272 | bytes 1576960 | tf_op jit(solution)/shard_map/reduce_sum | solution.py:34
  2.6 0.0 copy-start.5
  2.6 0.3 fusion.1.refs_3_
  2.9 0.8 slice.53
  3.7 2.9 %collective-permute-start.3 = (bf16[256,768]{1,0:T(8,128)(2,1)}, bf16[256,768]{1,0:T(8,128)(2,1)S(1)}, u32[]{:S(2)}, u32[]{:S(2)}) collective-permute-start(bf16[256,768]{1,0:T(8,128)(2,1)} %slice.53), channel_id=1, source_target_pairs={{0,1},{1,2},{2,3},{3,4},{4,5},{5,6},{6,7},{7,8},{8,9},{9,10},{10,1... | collective-permute-start | bytes 1179656 | tf_op jit(solution)/shard_map/ppermute | solution.py:19
  6.6 3.4 %collective-permute-start.2 = (bf16[256,768]{1,0:T(8,128)(2,1)}, bf16[256,768]{1,0:T(8,128)(2,1)S(1)}, u32[]{:S(2)}, u32[]{:S(2)}) collective-permute-start(bf16[256,768]{1,0:T(8,128)(2,1)} %slice.53), channel_id=1, source_target_pairs={{0,31},{1,0},{2,1},{3,2},{4,3},{5,4},{6,5},{7,6},{8,7},{9,8},{10,9... | collective-permute-start | bytes 1179656 | tf_op jit(solution)/shard_map/ppermute | solution.py:19
  10.1 0.2 fusion.3
  10.2 0.7 fusion.2
  10.9 1.9 %fusion.16 = (f32[256,256]{1,0:T(8,128)S(1)}, f32[2,256,256]{2,1,0:T(8,128)S(1)}) fusion(f32[2,512,256]{2,1,0:T(8,128)S(1)} %bitcast.30), kind=kOutput, calls=%fused_computation.42 | convolution fusion | flops 805502976 | bytes 1835008 | tf_op jit(solution)/shard_map/lpr,lps->lrs/dot_general | solution.py:188
  12.9 0.1 collective-permute-start
  12.9 1.3 %fusion.15 = (bf16[512,768]{1,0:T(8,128)(2,1)}, bf16[512,768]{1,0:T(8,128)(2,1)}) fusion(bf16[1024,768]{1,0:T(8,128)(2,1)S(1)} %fusion.1.refs_3_), kind=kLoop, calls=%fused_computation.41 | loop fusion | bytes 3145728 | tf_op jit(solution)/shard_map/slice | solution.py:176
  14.2 0.8 slice_bitcast_fusion
  15.0 16.2 %collective-permute-done = f32[256,256]{1,0:T(8,128)S(1)} collective-permute-done((f32[256,256]{1,0:T(8,128)S(1)}, f32[256,256]{1,0:T(8,128)S(1)}, u32[]{:S(2)}, u32[]{:S(2)}) %collective-permute-start) | collective-permute-done | bytes 262176 | tf_op jit(solution)/shard_map/ppermute | solution.py:29
  31.2 0.8 add_multiply_fusion.1
  32.0 1.2 %collective-permute-start.1 = (f32[256,256]{1,0:T(8,128)}, f32[256,256]{1,0:T(8,128)}, u32[]{:S(2)}, u32[]{:S(2)}) collective-permute-start(f32[256,256]{1,0:T(8,128)} %add_multiply_fusion.1), channel_id=1, source_target_pairs={{0,2},{2,0},{1,3},{3,1},{4,6},{6,4},{5,7},{7,5},{8,10},{10,8},{9,1... | collective-permute-start | bytes 786440 | tf_op jit(solution)/shard_map/ppermute | solution.py:29
  33.2 1.1 slice.48
  34.3 0.1 fusion.13.picks_ref
  34.3 5.2 %collective-permute-done.1 = f32[256,256]{1,0:T(8,128)} collective-permute-done((f32[256,256]{1,0:T(8,128)}, f32[256,256]{1,0:T(8,128)}, u32[]{:S(2)}, u32[]{:S(2)}) %collective-permute-start.1) | collective-permute-done | bytes 262176 | tf_op jit(solution)/shard_map/ppermute | solution.py:29
  39.5 1.1 add_multiply_fusion
  40.6 0.4 collective-permute-start.4
  41.0 4.1 %collective-permute-start.7 = (bf16[512,768]{1,0:T(8,128)(2,1)}, bf16[512,768]{1,0:T(8,128)(2,1)S(1)}, u32[]{:S(2)}, u32[]{:S(2)}) collective-permute-start(bf16[512,768]{1,0:T(8,128)(2,1)} %get-tuple-element.24), channel_id=1, source_target_pairs={{0,30},{1,31},{2,0},{3,1},{4,2},{5,3},{6,4},{7,5},{8,6},{9,7},{10,... | collective-permute-start | bytes 2359304 | tf_op jit(solution)/shard_map/ppermute | solution.py:19
  45.1 1.4 %collective-permute-start.5 = (bf16[768,768]{1,0:T(8,128)(2,1)}, bf16[768,768]{1,0:T(8,128)(2,1)S(1)}, u32[]{:S(2)}, u32[]{:S(2)}) collective-permute-start(bf16[768,768]{1,0:T(8,128)(2,1)} %slice.48), channel_id=1, source_target_pairs={{0,1},{1,2},{2,3},{3,4},{4,5},{5,6},{6,7},{7,8},{8,9},{9,10},{10,1... | collective-permute-start | bytes 3538952 | tf_op jit(solution)/shard_map/ppermute | solution.py:19
  46.5 3.9 %collective-permute-start.6 = (bf16[768,768]{1,0:T(8,128)(2,1)}, bf16[768,768]{1,0:T(8,128)(2,1)S(1)}, u32[]{:S(2)}, u32[]{:S(2)}) collective-permute-start(bf16[768,768]{1,0:T(8,128)(2,1)} %slice.48), channel_id=1, source_target_pairs={{0,31},{1,0},{2,1},{3,2},{4,3},{5,4},{6,5},{7,6},{8,7},{9,8},{10,9... | collective-permute-start | bytes 3538952 | tf_op jit(solution)/shard_map/ppermute | solution.py:19
  50.4 1.0 bitcast_dynamic-update-slice_fusion.6
  51.4 1.0 bitcast_dynamic-update-slice_fusion.5
  52.4 1.0 bitcast_dynamic-update-slice_fusion.2
  53.4 1.0 bitcast_dynamic-update-slice_fusion.1
  54.4 46.3 %factor.1 = (f32[7,256,256]{2,1,0:T(8,128)S(1)}, f32[7,256,256]{2,1,0:T(8,128)S(1)}) custom-call(f32[7,256,256]{2,1,0:T(8,128)S(1)} %bitcast_dynamic-update-slice_fusion.grams_ref), custom_call_target="tpu_custom_call" | custom-call | flops 40000000000 | bytes 8000000 | tf_op jit(solution)/shard_map/factor/pallas_call | solution.py:100
  100.7 1.5 %convolution_bitcast_fusion = f32[1,2,256,256]{3,2,1,0:T(8,128)} fusion(f32[7,256,256]{2,1,0:T(8,128)S(1)} %get-tuple-element.33, f32[7,256,256]{2,1,0:T(8,128)S(1)} %get-tuple-element.32), kind=kOutput, calls=%fused_computation.8 | convolution fusion | flops 402653184 | bytes 1572864 | tf_op jit(solution)/shard_map/tij,tkj->tik/dot_general | solution.py:209
  102.2 1.5 %convolution_bitcast_fusion.1 = f32[1,2,256,256]{3,2,1,0:T(8,128)} fusion(f32[7,256,256]{2,1,0:T(8,128)S(1)} %get-tuple-element.32, f32[7,256,256]{2,1,0:T(8,128)S(1)} %get-tuple-element.33), kind=kOutput, calls=%fused_computation.9 | convolution fusion | flops 402653184 | bytes 1572864 | tf_op jit(solution)/shard_map/tij,tkj->tik/dot_general | solution.py:208
  103.7 1.9 %convolution_convert_fusion = bf16[2,512,256]{2,1,0:T(8,128)(2,1)} fusion(f32[2,512,256]{2,1,0:T(8,128)S(1)} %bitcast.31, f32[7,256,256]{2,1,0:T(8,128)S(1)} %get-tuple-element.32), kind=kOutput, calls=%fused_computation.6 | convolution fusion | flops 805568512 | bytes 2097152 | tf_op jit(solution)/shard_map/lpr,lsr->lps/dot_general | solution.py:203
  105.6 8.1 %near.1 = f32[1024,4,512]{2,1,0:T(4,128)} custom-call(s32[2,4]{1,0:T(2,128)S(1)} %fusion.13.picks_ref, bf16[512,768]{1,0:T(8,128)(2,1)S(1)} %collective-permute-done.4.refs_0_, bf16[256,768]{1,0:T(8,128)(2,1)S(1)} %collective-permute-done.3.refs_1_, bf16[768,768]{1,0:T(8,128)(2,1)S(1)} %collective-permute-done.5.refs_2_, ...), custom_call_target="tpu_custom_call" | custom-call | flops 4000000000 | bytes 16000000 | tf_op jit(solution)/shard_map/near/pallas_call | solution.py:143
  (26 shorter events, 0.1 us)
Async XLA Ops:
  0.6 1.9 %copy-start = (bf16[1024,768]{1,0:T(8,128)(2,1)S(1)}, bf16[1024,768]{1,0:T(8,128)(2,1)}, u32[]{:S(2)}) copy-start(bf16[1024,768]{1,0:T(8,128)(2,1)} %param.3) | copy-start | bytes 4718596
  2.6 7.5 %copy-start.5 = (bf16[256,768]{1,0:T(8,128)(2,1)S(1)}, bf16[256,768]{1,0:T(8,128)(2,1)}, u32[]{:S(2)}) copy-start(bf16[256,768]{1,0:T(8,128)(2,1)} %param.4) | copy-start | bytes 1179652
  3.7 36.9 %collective-permute-start.3 = (bf16[256,768]{1,0:T(8,128)(2,1)}, bf16[256,768]{1,0:T(8,128)(2,1)S(1)}, u32[]{:S(2)}, u32[]{:S(2)}) collective-permute-start(bf16[256,768]{1,0:T(8,128)(2,1)} %slice.53), channel_id=1, source_target_pairs={{0,1},{1,2},{2,3},{3,4},{4,5},{5,6},{6,7},{7,8},{8,9},{9,10},{10,1... | collective-permute-start | bytes 1179656 | tf_op jit(solution)/shard_map/ppermute | solution.py:19
  6.6 33.9 %collective-permute-start.2 = (bf16[256,768]{1,0:T(8,128)(2,1)}, bf16[256,768]{1,0:T(8,128)(2,1)S(1)}, u32[]{:S(2)}, u32[]{:S(2)}) collective-permute-start(bf16[256,768]{1,0:T(8,128)(2,1)} %slice.53), channel_id=1, source_target_pairs={{0,31},{1,0},{2,1},{3,2},{4,3},{5,4},{6,5},{7,6},{8,7},{9,8},{10,9... | collective-permute-start | bytes 1179656 | tf_op jit(solution)/shard_map/ppermute | solution.py:19
  12.8 2.2 %copy-start.3 = (f32[256,256]{1,0:T(8,128)}, f32[256,256]{1,0:T(8,128)S(1)}, u32[]{:S(2)}) copy-start(f32[256,256]{1,0:T(8,128)S(1)} %broadcast_multiply_fusion) | copy-start | bytes 786436
  12.9 18.3 %collective-permute-start = (f32[256,256]{1,0:T(8,128)S(1)}, f32[256,256]{1,0:T(8,128)S(1)}, u32[]{:S(2)}, u32[]{:S(2)}) collective-permute-start(f32[256,256]{1,0:T(8,128)S(1)} %broadcast_multiply_fusion), channel_id=1, source_target_pairs={{0,1},{1,0},{2,3},{3,2},{4,5},{5,4},{6,7},{7,6},{8,9},{9,8},{10,11... | collective-permute-start | bytes 786440 | tf_op jit(solution)/shard_map/ppermute | solution.py:29
  15.0 19.2 %copy-start.6 = (s32[2,4]{1,0:T(2,128)S(1)}, s32[2,4]{1,0:T(2,128)}, u32[]{:S(2)}) copy-start(s32[2,4]{1,0:T(2,128)} %param.5) | copy-start | bytes 100
  31.2 0.8 copy-start.1
  32.0 7.5 %collective-permute-start.1 = (f32[256,256]{1,0:T(8,128)}, f32[256,256]{1,0:T(8,128)}, u32[]{:S(2)}, u32[]{:S(2)}) collective-permute-start(f32[256,256]{1,0:T(8,128)} %add_multiply_fusion.1), channel_id=1, source_target_pairs={{0,2},{2,0},{1,3},{3,1},{4,6},{6,4},{5,7},{7,5},{8,10},{10,8},{9,1... | collective-permute-start | bytes 786440 | tf_op jit(solution)/shard_map/ppermute | solution.py:29
  34.3 18.1 %copy-start.4 = (f32[256,256]{1,0:T(8,128)S(1)}, f32[256,256]{1,0:T(8,128)}, u32[]{:S(2)}) copy-start(f32[256,256]{1,0:T(8,128)} %copy-done.3) | copy-start | bytes 786436
  34.3 18.1 %copy-start.2 = (f32[256,256]{1,0:T(8,128)S(1)}, f32[256,256]{1,0:T(8,128)}, u32[]{:S(2)}) copy-start(f32[256,256]{1,0:T(8,128)} %copy-done.1) | copy-start | bytes 786436
  40.6 65.0 %collective-permute-start.4 = (bf16[512,768]{1,0:T(8,128)(2,1)}, bf16[512,768]{1,0:T(8,128)(2,1)S(1)}, u32[]{:S(2)}, u32[]{:S(2)}) collective-permute-start(bf16[512,768]{1,0:T(8,128)(2,1)} %get-tuple-element.19), channel_id=1, source_target_pairs={{0,2},{1,3},{2,4},{3,5},{4,6},{5,7},{6,8},{7,9},{8,10},{9,11},{10,... | collective-permute-start | bytes 2359304 | tf_op jit(solution)/shard_map/ppermute | solution.py:19
  41.0 64.6 %collective-permute-start.7 = (bf16[512,768]{1,0:T(8,128)(2,1)}, bf16[512,768]{1,0:T(8,128)(2,1)S(1)}, u32[]{:S(2)}, u32[]{:S(2)}) collective-permute-start(bf16[512,768]{1,0:T(8,128)(2,1)} %get-tuple-element.24), channel_id=1, source_target_pairs={{0,30},{1,31},{2,0},{3,1},{4,2},{5,3},{6,4},{7,5},{8,6},{9,7},{10,... | collective-permute-start | bytes 2359304 | tf_op jit(solution)/shard_map/ppermute | solution.py:19
  45.1 60.5 %collective-permute-start.5 = (bf16[768,768]{1,0:T(8,128)(2,1)}, bf16[768,768]{1,0:T(8,128)(2,1)S(1)}, u32[]{:S(2)}, u32[]{:S(2)}) collective-permute-start(bf16[768,768]{1,0:T(8,128)(2,1)} %slice.48), channel_id=1, source_target_pairs={{0,1},{1,2},{2,3},{3,4},{4,5},{5,6},{6,7},{7,8},{8,9},{9,10},{10,1... | collective-permute-start | bytes 3538952 | tf_op jit(solution)/shard_map/ppermute | solution.py:19
  46.5 59.1 %collective-permute-start.6 = (bf16[768,768]{1,0:T(8,128)(2,1)}, bf16[768,768]{1,0:T(8,128)(2,1)S(1)}, u32[]{:S(2)}, u32[]{:S(2)}) collective-permute-start(bf16[768,768]{1,0:T(8,128)(2,1)} %slice.48), channel_id=1, source_target_pairs={{0,31},{1,0},{2,1},{3,2},{4,3},{5,4},{6,5},{7,6},{8,7},{9,8},{10,9... | collective-permute-start | bytes 3538952 | tf_op jit(solution)/shard_map/ppermute | solution.py:19

commit v6 on v5

--- a/solution.py
+++ b/solution.py
@@ -45,12 +45,8 @@
 
 def factor_kernel(count, rank, grams_ref, upper_ref, inverse_ref, work, *blocks):
     b = PANEL
-    eye_row = lax.broadcasted_iota(jnp.int32, (rank, rank), 0)
-    eye_col = lax.broadcasted_iota(jnp.int32, (rank, rank), 1)
-    eye = jnp.where(eye_row == eye_col, 1.0, 0.0).astype(jnp.float32)
     for m in range(count):
-        work[m, :, :rank] = grams_ref[m]
-        work[m, :, rank:] = eye
+        work[m] = grams_ref[m]
     for block in blocks:
         block[...] = jnp.ones_like(block)
     lane = lax.broadcasted_iota(jnp.int32, (b, 128), 1)
@@ -59,10 +55,12 @@
     panel_row = lax.broadcasted_iota(jnp.int32, (b, rank), 0)
     panel_col = lax.broadcasted_iota(jnp.int32, (b, rank), 1)
 
+    all_col = lax.broadcasted_iota(jnp.int32, (rank, rank), 1)
+
     def panel(step, carry):
         start = pl.multiple_of(step * b, b)
         for m in range(count):
-            rows = work[m, pl.ds(start, b), :rank]
+            rows = work[m, pl.ds(start, b), :]
             rolled = pltpu.roll(rows, rank - start, 1)[:, :128]
             blocks[m // 8][pl.ds(m % 8, b, stride=8), :] = jnp.where(lane < b, rolled, unit_part)
         for block in blocks:
@@ -74,23 +72,24 @@
                     v[i] = v[i] - jnp.broadcast_to(v[k][:, i:i + 1], (8, 128)) * scaled
                 block[k * 8:(k + 1) * 8, :] = v[k] * lax.rsqrt(pivot)
         for m in range(count):
-            small = blocks[m // 8][pl.ds(m % 8, b, stride=8), :][:, b:2 * b]
+            strip = blocks[m // 8][pl.ds(m % 8, b, stride=8), :]
+            small = strip[:, b:2 * b]
             reduced = jnp.dot(small, work[m, pl.ds(start, b), :], precision=HIGHEST, preferred_element_type=jnp.float32)
-            left = jnp.where(panel_col >= start + panel_row, reduced[:, :rank], 0.0)
-            work[m, pl.ds(start, b), :rank] = left
-            work[m, pl.ds(start, b), rank:] = reduced[:, rank:]
-            full = jnp.concatenate([left, reduced[:, rank:]], axis=1)
+            left = jnp.where(panel_col >= start + panel_row, reduced, 0.0)
+            upper_ref[m, pl.ds(start, b), :] = left
+            placed = pltpu.roll(jnp.concatenate([strip] + [jnp.zeros_like(strip)] * (rank // 128 - 1), axis=1), lax.rem(start + rank - b, rank), 1)
+            done = jnp.where(panel_col < start, reduced, jnp.where(panel_col <= start + panel_row, placed, 0.0))
+            inverse_ref[m, pl.ds(start, b), :] = done
+            full = jnp.where(panel_col < start + b, done, reduced)
             y1, y2, y3 = split3(full)
-            x1, x2, x3 = split3(jnp.where(panel_col >= start + b, left, 0.0))
+            x1, x2, x3 = split3(jnp.where(panel_col >= start + b, reduced, 0.0))
             lhs = jnp.concatenate([x1, x1, x2, x2, x1, x3], axis=0)
             rhs = jnp.concatenate([y1, y2, y1, y2, y3, y1], axis=0)
-            work[m] = work[m] - lax.dot_general(lhs, rhs, (((0,), (0,)), ((), ())), preferred_element_type=jnp.float32)
+            kept = jnp.where((all_col >= start) & (all_col < start + b), 0.0, work[m])
+            work[m] = kept - lax.dot_general(lhs, rhs, (((0,), (0,)), ((), ())), preferred_element_type=jnp.float32)
         return carry
 
     lax.fori_loop(0, rank // b, panel, 0)
-    for m in range(count):
-        upper_ref[m] = work[m, :, :rank]
-        inverse_ref[m] = work[m, :, rank:]
 
 
 def factors_of(grams):
@@ -102,7 +101,7 @@
         out_shape=(shape, shape),
         in_specs=[vmem],
         out_specs=(vmem, vmem),
-        scratch_shapes=[pltpu.VMEM((count, rank, 2 * rank), jnp.float32)]
+        scratch_shapes=[pltpu.VMEM((count, rank, rank), jnp.float32)]
         + [pltpu.VMEM((8 * PANEL, 128), jnp.float32)] * ((count + 7) // 8),
         compiler_params=pltpu.CompilerParams(vmem_limit_bytes=40 << 20),
         cost_estimate=pl.CostEstimate(flops=40_000_000_000, bytes_accessed=8_000_000, transcendentals=0),
@@ -174,7 +173,7 @@
         count = min(leaves_dev, reach - (step - 1) * leaves_dev)
         plan.append((leaves[leaves_dev - count :], step))
         plan.append((leaves[:count], -step))
-    share = LEAF // 2
+    share = LEAF * 3 // 8
     first = {}
     late = []
     for piece, step in plan:

time: 114 us -> 113 us (level)
  waiting for transfers between devices: 21.3 us -> 26.5 us
  local copies, waits for them, and re-layouts: 7.9 us -> 4.73 us
  Pallas kernels: 54.4 us -> 52 us
    ppermute x6, waiting for transfers between devices: 0.02 us -> 8.68 us  [from_behind(): return lax.ppermute(value, axis, pairs)]
    ppermute x2, waiting for transfers between devices: 21.3 us -> 17.9 us  [from_partner(): return lax.ppermute(block, axis, route)]
    pallas_call x1, Pallas kernels: 46.3 us -> 44 us  [factors_of(): pl.pallas_call(functools.partial(factor_kernel, count, rank), out_shape=(...]
    unnamed x20 -> x28, local copies, waits for them, and re-layouts: 3.94 us -> 1.79 us
  transfers between devices with their start and end apart: 8 -> 8, of which waited for: 2 -> 4; matrix products, arithmetic and copies ran while one was open for 15% -> 11% of each run, Pallas kernels for 41% -> 39%
where the time goes in v6:
time: 113 us
  Pallas kernels  52 us (46%)
  waiting for transfers between devices  26.5 us (23%)
  starting transfers between devices  17.5 us (15%)
  matrix products  7.38 us (7%)
  local copies, waits for them, and re-layouts  4.73 us (4%)
  other arithmetic  3.5 us (3%)
    pallas_call x1, Pallas kernels, factors_of(): pl.pallas_call(functools.partial(factor_kernel, count, rank), out_shape=(...  44 us
    ppermute x2, waiting for transfers between devices, from_partner(): return lax.ppermute(block, axis, route)  17.9 us
    ppermute x6, starting transfers between devices, from_behind(): return lax.ppermute(value, axis, pairs)  16.2 us
    ppermute x6, waiting for transfers between devices, from_behind(): return lax.ppermute(value, axis, pairs)  8.68 us
    pallas_call x1, Pallas kernels, near_field(): pl.pallas_call(functools.partial(near_kernel, beta), out_shape=jax.ShapeD...  8.06 us
  transfers between devices with their start and end apart: 8, of which 4 were waited for; matrix products, arithmetic and copies ran while one was open for 11% of the time, Pallas kernels for 39%

profile of v6, /device:TPU:0, one launch (start us, length us, event | category | flops | bytes accessed | tf_op | source)
XLA Modules:
  0.0 112.5 jit_solution(1239254957838385202)
XLA Ops:
  0.6 1.9 %fusion = f32[1024]{0:T(1024)S(1)} fusion(bf16[1024,768]{1,0:T(8,128)(2,1)} %param.3), kind=kLoop, calls=%fused_computation.2 | loop fusion | flops 2358272 | bytes 1576960 | tf_op jit(solution)/shard_map/reduce_sum | solution.py:34
  2.6 0.0 copy-start.9
  2.6 0.3 fusion.1.refs_3_
  2.9 0.7 slice.53
  3.6 2.9 %collective-permute-start.3 = (bf16[192,768]{1,0:T(8,128)(2,1)}, bf16[192,768]{1,0:T(8,128)(2,1)S(1)}, u32[]{:S(2)}, u32[]{:S(2)}) collective-permute-start(bf16[192,768]{1,0:T(8,128)(2,1)} %slice.53), channel_id=1, source_target_pairs={{0,1},{1,2},{2,3},{3,4},{4,5},{5,6},{6,7},{7,8},{8,9},{9,10},{10,1... | collective-permute-start | bytes 884744 | tf_op jit(solution)/shard_map/ppermute | solution.py:19
  6.6 3.4 %collective-permute-start.2 = (bf16[192,768]{1,0:T(8,128)(2,1)}, bf16[192,768]{1,0:T(8,128)(2,1)S(1)}, u32[]{:S(2)}, u32[]{:S(2)}) collective-permute-start(bf16[192,768]{1,0:T(8,128)(2,1)} %slice.53), channel_id=1, source_target_pairs={{0,31},{1,0},{2,1},{3,2},{4,3},{5,4},{6,5},{7,6},{8,7},{9,8},{10,9... | collective-permute-start | bytes 884744 | tf_op jit(solution)/shard_map/ppermute | solution.py:19
  10.0 0.2 fusion.3
  10.2 0.7 fusion.2
  10.9 1.9 %fusion.16 = (f32[256,256]{1,0:T(8,128)S(1)}, f32[2,256,256]{2,1,0:T(8,128)S(1)}) fusion(f32[2,512,256]{2,1,0:T(8,128)S(1)} %bitcast.30), kind=kOutput, calls=%fused_computation.42 | convolution fusion | flops 805502976 | bytes 1835008 | tf_op jit(solution)/shard_map/lpr,lps->lrs/dot_general | solution.py:187
  12.8 0.0 copy-start.10
  12.8 0.1 collective-permute-start
  12.9 1.3 %fusion.15 = (bf16[512,768]{1,0:T(8,128)(2,1)}, bf16[512,768]{1,0:T(8,128)(2,1)}) fusion(bf16[1024,768]{1,0:T(8,128)(2,1)S(1)} %fusion.1.refs_3_), kind=kLoop, calls=%fused_computation.41 | loop fusion | bytes 3145728 | tf_op jit(solution)/shard_map/slice | solution.py:175
  14.2 0.8 slice_bitcast_fusion
  15.0 11.9 %collective-permute-done = f32[256,256]{1,0:T(8,128)S(1)} collective-permute-done((f32[256,256]{1,0:T(8,128)S(1)}, f32[256,256]{1,0:T(8,128)S(1)}, u32[]{:S(2)}, u32[]{:S(2)}) %collective-permute-start) | collective-permute-done | bytes 262176 | tf_op jit(solution)/shard_map/ppermute | solution.py:29
  27.0 0.7 copy-done.1
  27.7 1.2 %collective-permute-start.1 = (f32[256,256]{1,0:T(8,128)S(1)}, f32[256,256]{1,0:T(8,128)}, u32[]{:S(2)}, u32[]{:S(2)}) collective-permute-start(f32[256,256]{1,0:T(8,128)S(1)} %add_multiply_fusion.1), channel_id=1, source_target_pairs={{0,2},{2,0},{1,3},{3,1},{4,6},{6,4},{5,7},{7,5},{8,10},{10,8},{9,1... | collective-permute-start | bytes 786440 | tf_op jit(solution)/shard_map/ppermute | solution.py:29
  28.9 0.1 fusion.13.picks_ref
  28.9 0.1 slice.48
  29.0 5.9 %collective-permute-done.1 = f32[256,256]{1,0:T(8,128)} collective-permute-done((f32[256,256]{1,0:T(8,128)S(1)}, f32[256,256]{1,0:T(8,128)}, u32[]{:S(2)}, u32[]{:S(2)}) %collective-permute-start.1) | collective-permute-done | bytes 262176 | tf_op jit(solution)/shard_map/ppermute | solution.py:29
  34.9 1.0 add_multiply_fusion
  36.0 0.4 collective-permute-start.4
  36.4 4.1 %collective-permute-start.7 = (bf16[512,768]{1,0:T(8,128)(2,1)S(1)}, bf16[512,768]{1,0:T(8,128)(2,1)S(1)}, u32[]{:S(2)}, u32[]{:S(2)}) collective-permute-start(bf16[512,768]{1,0:T(8,128)(2,1)S(1)} %copy-done.7), channel_id=1, source_target_pairs={{0,30},{1,31},{2,0},{3,1},{4,2},{5,3},{6,4},{7,5},{8,6},{9,7},{10,... | collective-permute-start | bytes 2359304 | tf_op jit(solution)/shard_map/ppermute | solution.py:19
  40.5 1.4 %collective-permute-start.5 = (bf16[832,768]{1,0:T(8,128)(2,1)S(1)}, bf16[832,768]{1,0:T(8,128)(2,1)S(1)}, u32[]{:S(2)}, u32[]{:S(2)}) collective-permute-start(bf16[832,768]{1,0:T(8,128)(2,1)S(1)} %slice.48), channel_id=1, source_target_pairs={{0,1},{1,2},{2,3},{3,4},{4,5},{5,6},{6,7},{7,8},{8,9},{9,10},{10,1... | collective-permute-start | bytes 3833864 | tf_op jit(solution)/shard_map/ppermute | solution.py:19
  41.9 3.9 %collective-permute-start.6 = (bf16[832,768]{1,0:T(8,128)(2,1)S(1)}, bf16[832,768]{1,0:T(8,128)(2,1)S(1)}, u32[]{:S(2)}, u32[]{:S(2)}) collective-permute-start(bf16[832,768]{1,0:T(8,128)(2,1)S(1)} %slice.48), channel_id=1, source_target_pairs={{0,31},{1,0},{2,1},{3,2},{4,3},{5,4},{6,5},{7,6},{8,7},{9,8},{10,9... | collective-permute-start | bytes 3833864 | tf_op jit(solution)/shard_map/ppermute | solution.py:19
  46.0 1.0 bitcast_dynamic-update-slice_fusion.1
  47.0 44.0 %factor.1 = (f32[7,256,256]{2,1,0:T(8,128)S(1)}, f32[7,256,256]{2,1,0:T(8,128)S(1)}) custom-call(f32[7,256,256]{2,1,0:T(8,128)S(1)} %bitcast_dynamic-update-slice_fusion.grams_ref), custom_call_target="tpu_custom_call" | custom-call | flops 40000000000 | bytes 8000000 | tf_op jit(solution)/shard_map/factor/pallas_call | solution.py:99
  91.0 1.5 %convolution_bitcast_fusion = f32[1,2,256,256]{3,2,1,0:T(8,128)} fusion(f32[7,256,256]{2,1,0:T(8,128)S(1)} %get-tuple-element.33, f32[7,256,256]{2,1,0:T(8,128)S(1)} %get-tuple-element.32), kind=kOutput, calls=%fused_computation.8 | convolution fusion | flops 402653184 | bytes 1572864 | tf_op jit(solution)/shard_map/tij,tkj->tik/dot_general | solution.py:208
  92.4 1.5 %convolution_bitcast_fusion.1 = f32[1,2,256,256]{3,2,1,0:T(8,128)} fusion(f32[7,256,256]{2,1,0:T(8,128)S(1)} %get-tuple-element.32, f32[7,256,256]{2,1,0:T(8,128)S(1)} %get-tuple-element.33), kind=kOutput, calls=%fused_computation.9 | convolution fusion | flops 402653184 | bytes 1572864 | tf_op jit(solution)/shard_map/tij,tkj->tik/dot_general | solution.py:207
  93.9 1.9 %convolution_convert_fusion = bf16[2,512,256]{2,1,0:T(8,128)(2,1)} fusion(f32[2,512,256]{2,1,0:T(8,128)S(1)} %bitcast.31, f32[7,256,256]{2,1,0:T(8,128)S(1)} %get-tuple-element.32), kind=kOutput, calls=%fused_computation.6 | convolution fusion | flops 805568512 | bytes 2097152 | tf_op jit(solution)/shard_map/lpr,lsr->lps/dot_general | solution.py:202
  95.8 3.2 %collective-permute-done.7.refs_6_ = bf16[512,768]{1,0:T(8,128)(2,1)S(1)} collective-permute-done((bf16[512,768]{1,0:T(8,128)(2,1)S(1)}, bf16[512,768]{1,0:T(8,128)(2,1)S(1)}, u32[]{:S(2)}, u32[]{:S(2)}) %collective-permute-start.7) | collective-permute-done | bytes 786464 | tf_op jit(solution)/shard_map/ppermute | solution.py:19
  99.0 5.4 %collective-permute-done.6.refs_5_ = bf16[832,768]{1,0:T(8,128)(2,1)S(1)} collective-permute-done((bf16[832,768]{1,0:T(8,128)(2,1)S(1)}, bf16[832,768]{1,0:T(8,128)(2,1)S(1)}, u32[]{:S(2)}, u32[]{:S(2)}) %collective-permute-start.6) | collective-permute-done | bytes 1277984 | tf_op jit(solution)/shard_map/ppermute | solution.py:19
  104.5 8.1 %near.1 = f32[1024,4,512]{2,1,0:T(4,128)} custom-call(s32[2,4]{1,0:T(2,128)S(1)} %fusion.13.picks_ref, bf16[512,768]{1,0:T(8,128)(2,1)S(1)} %collective-permute-done.4.refs_0_, bf16[192,768]{1,0:T(8,128)(2,1)S(1)} %collective-permute-done.3.refs_1_, bf16[832,768]{1,0:T(8,128)(2,1)S(1)} %collective-permute-done.5.refs_2_, ...), custom_call_target="tpu_custom_call" | custom-call | flops 4000000000 | bytes 16000000 | tf_op jit(solution)/shard_map/near/pallas_call | solution.py:142
  (34 shorter events, 0.2 us)
Async XLA Ops:
  0.6 1.9 %copy-start = (bf16[1024,768]{1,0:T(8,128)(2,1)S(1)}, bf16[1024,768]{1,0:T(8,128)(2,1)}, u32[]{:S(2)}) copy-start(bf16[1024,768]{1,0:T(8,128)(2,1)} %param.3) | copy-start | bytes 4718596
  2.6 7.5 %copy-start.9 = (bf16[256,768]{1,0:T(8,128)(2,1)S(1)}, bf16[256,768]{1,0:T(8,128)(2,1)}, u32[]{:S(2)}) copy-start(bf16[256,768]{1,0:T(8,128)(2,1)} %param.4) | copy-start | bytes 1179652
  3.6 32.3 %collective-permute-start.3 = (bf16[192,768]{1,0:T(8,128)(2,1)}, bf16[192,768]{1,0:T(8,128)(2,1)S(1)}, u32[]{:S(2)}, u32[]{:S(2)}) collective-permute-start(bf16[192,768]{1,0:T(8,128)(2,1)} %slice.53), channel_id=1, source_target_pairs={{0,1},{1,2},{2,3},{3,4},{4,5},{5,6},{6,7},{7,8},{8,9},{9,10},{10,1... | collective-permute-start | bytes 884744 | tf_op jit(solution)/shard_map/ppermute | solution.py:19
  6.6 29.4 %collective-permute-start.2 = (bf16[192,768]{1,0:T(8,128)(2,1)}, bf16[192,768]{1,0:T(8,128)(2,1)S(1)}, u32[]{:S(2)}, u32[]{:S(2)}) collective-permute-start(bf16[192,768]{1,0:T(8,128)(2,1)} %slice.53), channel_id=1, source_target_pairs={{0,31},{1,0},{2,1},{3,2},{4,3},{5,4},{6,5},{7,6},{8,7},{9,8},{10,9... | collective-permute-start | bytes 884744 | tf_op jit(solution)/shard_map/ppermute | solution.py:19
  12.8 2.2 %copy-start.3 = (f32[256,256]{1,0:T(8,128)}, f32[256,256]{1,0:T(8,128)S(1)}, u32[]{:S(2)}) copy-start(f32[256,256]{1,0:T(8,128)S(1)} %broadcast_multiply_fusion) | copy-start | bytes 786436
  12.8 16.0 %copy-start.10 = (s32[2,4]{1,0:T(2,128)S(1)}, s32[2,4]{1,0:T(2,128)}, u32[]{:S(2)}) copy-start(s32[2,4]{1,0:T(2,128)} %param.5) | copy-start | bytes 100
  12.8 14.1 %collective-permute-start = (f32[256,256]{1,0:T(8,128)S(1)}, f32[256,256]{1,0:T(8,128)S(1)}, u32[]{:S(2)}, u32[]{:S(2)}) collective-permute-start(f32[256,256]{1,0:T(8,128)S(1)} %broadcast_multiply_fusion), channel_id=1, source_target_pairs={{0,1},{1,0},{2,3},{3,2},{4,5},{5,4},{6,7},{7,6},{8,9},{9,8},{10,11... | collective-permute-start | bytes 786440 | tf_op jit(solution)/shard_map/ppermute | solution.py:29
  26.9 0.7 copy-start.1
  27.7 7.3 %collective-permute-start.1 = (f32[256,256]{1,0:T(8,128)S(1)}, f32[256,256]{1,0:T(8,128)}, u32[]{:S(2)}, u32[]{:S(2)}) collective-permute-start(f32[256,256]{1,0:T(8,128)S(1)} %add_multiply_fusion.1), channel_id=1, source_target_pairs={{0,2},{2,0},{1,3},{3,1},{4,6},{6,4},{5,7},{7,5},{8,10},{10,8},{9,1... | collective-permute-start | bytes 786440 | tf_op jit(solution)/shard_map/ppermute | solution.py:29
  28.8 7.1 %copy-start.8 = (bf16[512,768]{1,0:T(8,128)(2,1)S(1)}, bf16[512,768]{1,0:T(8,128)(2,1)}, u32[]{:S(2)}) copy-start(bf16[512,768]{1,0:T(8,128)(2,1)} %get-tuple-element.19) | copy-start | bytes 2359300
  28.8 7.6 %copy-start.7 = (bf16[512,768]{1,0:T(8,128)(2,1)S(1)}, bf16[512,768]{1,0:T(8,128)(2,1)}, u32[]{:S(2)}) copy-start(bf16[512,768]{1,0:T(8,128)(2,1)} %get-tuple-element.24) | copy-start | bytes 2359300
  28.8 17.0 %copy-start.6 = (f32[256,256]{1,0:T(8,128)S(1)}, f32[256,256]{1,0:T(8,128)}, u32[]{:S(2)}) copy-start(f32[256,256]{1,0:T(8,128)} %get-tuple-element.25) | copy-start | bytes 786436
  28.9 16.9 %copy-start.5 = (f32[256,256]{1,0:T(8,128)S(1)}, f32[256,256]{1,0:T(8,128)}, u32[]{:S(2)}) copy-start(f32[256,256]{1,0:T(8,128)} %get-tuple-element.26) | copy-start | bytes 786436
  28.9 16.9 %copy-start.4 = (f32[256,256]{1,0:T(8,128)S(1)}, f32[256,256]{1,0:T(8,128)}, u32[]{:S(2)}) copy-start(f32[256,256]{1,0:T(8,128)} %copy-done.3) | copy-start | bytes 786436
  28.9 17.0 %copy-start.2 = (f32[256,256]{1,0:T(8,128)S(1)}, f32[256,256]{1,0:T(8,128)}, u32[]{:S(2)}) copy-start(f32[256,256]{1,0:T(8,128)} %copy-done.1) | copy-start | bytes 786436
  36.0 59.8 %collective-permute-start.4 = (bf16[512,768]{1,0:T(8,128)(2,1)S(1)}, bf16[512,768]{1,0:T(8,128)(2,1)S(1)}, u32[]{:S(2)}, u32[]{:S(2)}) collective-permute-start(bf16[512,768]{1,0:T(8,128)(2,1)S(1)} %copy-done.8), channel_id=1, source_target_pairs={{0,2},{1,3},{2,4},{3,5},{4,6},{5,7},{6,8},{7,9},{8,10},{9,11},{10,... | collective-permute-start | bytes 2359304 | tf_op jit(solution)/shard_map/ppermute | solution.py:19
  36.4 62.6 %collective-permute-start.7 = (bf16[512,768]{1,0:T(8,128)(2,1)S(1)}, bf16[512,768]{1,0:T(8,128)(2,1)S(1)}, u32[]{:S(2)}, u32[]{:S(2)}) collective-permute-start(bf16[512,768]{1,0:T(8,128)(2,1)S(1)} %copy-done.7), channel_id=1, source_target_pairs={{0,30},{1,31},{2,0},{3,1},{4,2},{5,3},{6,4},{7,5},{8,6},{9,7},{10,... | collective-permute-start | bytes 2359304 | tf_op jit(solution)/shard_map/ppermute | solution.py:19
  40.5 58.6 %collective-permute-start.5 = (bf16[832,768]{1,0:T(8,128)(2,1)S(1)}, bf16[832,768]{1,0:T(8,128)(2,1)S(1)}, u32[]{:S(2)}, u32[]{:S(2)}) collective-permute-start(bf16[832,768]{1,0:T(8,128)(2,1)S(1)} %slice.48), channel_id=1, source_target_pairs={{0,1},{1,2},{2,3},{3,4},{4,5},{5,6},{6,7},{7,8},{8,9},{9,10},{10,1... | collective-permute-start | bytes 3833864 | tf_op jit(solution)/shard_map/ppermute | solution.py:19
  41.9 62.6 %collective-permute-start.6 = (bf16[832,768]{1,0:T(8,128)(2,1)S(1)}, bf16[832,768]{1,0:T(8,128)(2,1)S(1)}, u32[]{:S(2)}, u32[]{:S(2)}) collective-permute-start(bf16[832,768]{1,0:T(8,128)(2,1)S(1)} %slice.48), channel_id=1, source_target_pairs={{0,31},{1,0},{2,1},{3,2},{4,3},{5,4},{6,5},{7,6},{8,7},{9,8},{10,9... | collective-permute-start | bytes 3833864 | tf_op jit(solution)/shard_map/ppermute | solution.py:19
